TPU v7x, 32 devices: a whole 2x2x4 slice. The times are simulated.
32 devices in a mesh: row: 8 (over y, x, core), col: 4 (over z).
Axes of the slice: x: 2, y: 2, z: 4, core: 2. Of those that a mesh axis runs over, the one named last changes fastest.
Arguments:
- object_re: float32 [3072, 2048], P('row', 'col'), may hold values from -6 to 6
- object_im: float32 [3072, 2048], P('row', 'col'), may hold values from -6 to 6
- probe_re: float32 [256, 256], replicated, may hold values from -6 to 6
- probe_im: float32 [256, 256], replicated, may hold values from -6 to 6
- frames: bfloat16 [8, 4, 8, 256, 256], P('row', 'col'), may hold values from 0.049804688 to 20
- counts: int32 [8, 4], P('row', 'col'), may hold values from 1 to 8, as said below
- offsets: int32 [8, 4, 8, 2], P('row', 'col'), may hold values from -32 to 288, as said below
- frame_index: int32 [8, 4, 8], P('row', 'col'), may hold values from 0 to 7
Outputs:
- new_re: float32 [3072, 2048], P('row', 'col')
- new_im: float32 [3072, 2048], P('row', 'col')
Inputs may be any that keep to these rules, and one draw needn't show every extreme that they name: `counts`: in every draw some tile has 8 positions and some tile has one. Row offsets are -32 plus multiples of 16, at most 160; column offsets likewise, at most 288; in every draw some live position has both offsets at the lowest value and some has both at the highest.
All inputs are finite; a program needn't handle non-finite values.
Results may differ from a plain program's by a relative error of at most 0.0003.
Values sent between devices are 32-bit elements; how exact they have to be, the bound alone decides.
No kernel may reach another device: no remote copies, remote signals or barrier semaphores. Data moves between devices by JAX's collectives and lax.ppermute only.
A program may use at most 64 MiB of HBM per device.

v0:
```python
import math

import jax
import jax.numpy as jnp
from jax import lax
from jax.sharding import PartitionSpec as P

P_SIZE = 256
HALO = 32


floor_amp = 0.5
ridge = 1.0


def padded_2(cells, sides, width):
    for axis, dim in sides:
        count = lax.axis_size(axis)
        ends = count - 1
        head = lax.slice_in_dim(cells, 0, width, axis=dim)
        tail = lax.slice_in_dim(cells, cells.shape[dim] - width, cells.shape[dim], axis=dim)
        cells = jnp.concatenate(
            [
                lax.ppermute(tail, axis, [(i, (i + 1) % count) for i in range(ends)]),
                cells,
                lax.ppermute(head, axis, [((i + 1) % count, i) for i in range(ends)]),
            ],
            axis=dim,
        )
    return cells


def passed_along(shard, axis, by):
    devices = lax.axis_size(axis)
    pairs = [(i, i + by) for i in range(devices) if 0 <= i + by < devices]
    return lax.ppermute(shard, axis, pairs)


def transform_tables(length):
    index = jnp.arange(length, dtype=jnp.int32)
    phase = index[:, None] * index[None, :] % length
    angle = 2.0 * math.pi / length * phase.astype(jnp.float32)
    factor = 1.0 / math.sqrt(length)
    return (jnp.cos(angle) * factor, -jnp.sin(angle) * factor)


def complex_dot(left_re, left_im, right_re, right_im):
    highest = lax.Precision.HIGHEST
    first = jnp.dot(left_re, right_re, precision=highest, preferred_element_type=jnp.float32)
    second = jnp.dot(left_im, right_im, precision=highest, preferred_element_type=jnp.float32)
    third = jnp.dot(
        left_re + left_im,
        right_re + right_im,
        precision=highest,
        preferred_element_type=jnp.float32,
    )
    return (first - second, third - first - second)


def slot_gradient(patch, frame, probe_re, probe_im, table_re, table_im):
    exit_re = probe_re * patch[0] - probe_im * patch[1]
    exit_im = probe_re * patch[1] + probe_im * patch[0]
    half_re, half_im = complex_dot(exit_re, exit_im, table_re, table_im)
    far_re, far_im = complex_dot(table_re, table_im, half_re, half_im)
    amplitude = jnp.sqrt(far_re * far_re + far_im * far_im)
    factor = 1.0 - jnp.sqrt(frame.astype(jnp.float32)) / jnp.maximum(amplitude, floor_amp)
    res_re = far_re * factor
    res_im = far_im * factor
    half_re, half_im = complex_dot(res_re, res_im, table_re, -table_im)
    back_re, back_im = complex_dot(table_re, -table_im, half_re, half_im)
    grad_re = probe_re * back_re + probe_im * back_im
    grad_im = probe_re * back_im - probe_im * back_re
    return jnp.stack([grad_re, grad_im])


def window_start(places, slot):
    row_start = places[slot, 0] + HALO
    col_start = places[slot, 1] + HALO
    return (jnp.int32(0), row_start, col_start)


def add_window(acc, term, power, places, slot):
    start = window_start(places, slot)
    layers = acc.shape[0]
    full = jnp.concatenate([term, power[None]], axis=0)
    current = lax.dynamic_slice(acc, start, (layers, P_SIZE, P_SIZE))
    return lax.dynamic_update_slice(acc, current + full, start)


def shards(object_re, object_im, probe_re, probe_im, frames, counts, offsets, frame_index):
    tile_r, tile_c = object_re.shape
    table_re, table_im = transform_tables(P_SIZE)
    power = probe_re * probe_re + probe_im * probe_im
    stacked = jnp.stack([object_re, object_im])
    padded = padded_2(stacked, (("row", 1), ("col", 2)), HALO)
    places = offsets[0, 0]
    chosen = frame_index[0, 0]
    stored = frames[0, 0]
    count = counts[0, 0]
    layers = 3
    acc = jnp.zeros((layers, tile_r + 2 * HALO, tile_c + 2 * HALO), jnp.float32)

    def own_step(slot, acc):
        patch = lax.dynamic_slice(padded, window_start(places, slot), (2, P_SIZE, P_SIZE))
        frame = lax.dynamic_index_in_dim(stored, chosen[slot], 0, keepdims=False)
        term = slot_gradient(patch, frame, probe_re, probe_im, table_re, table_im)
        return add_window(acc, term, power, places, slot)

    acc = lax.fori_loop(0, count, own_step, acc)
    from_below = passed_along(acc[:, :HALO, :], "row", -1)
    from_above = passed_along(acc[:, HALO + tile_r :, :], "row", 1)
    acc = acc.at[:, tile_r : tile_r + HALO, :].add(from_below)
    acc = acc.at[:, HALO : 2 * HALO, :].add(from_above)
    middle = acc[:, HALO : HALO + tile_r, :]
    from_right = passed_along(middle[:, :, :HALO], "col", -1)
    from_left = passed_along(middle[:, :, HALO + tile_c :], "col", 1)
    middle = middle.at[:, :, tile_c : tile_c + HALO].add(from_right)
    middle = middle.at[:, :, HALO : 2 * HALO].add(from_left)
    inner = middle[:, :, HALO : HALO + tile_c]
    light = inner[2]
    denom = light + ridge
    return (object_re - inner[0] / denom, object_im - inner[1] / denom)


def solution(mesh):
    return jax.shard_map(
        shards,
        mesh=mesh,
        in_specs=(
            P("row", "col"),
            P("row", "col"),
            P(),
            P(),
            P("row", "col", None, None, None),
            P("row", "col"),
            P("row", "col", None, None),
            P("row", "col", None),
        ),
        out_specs=(P("row", "col"), P("row", "col")),
        check_vma=False,
    )
```

profile of v0, /device:TPU:20, one launch (start us, length us, event | category | flops | bytes accessed | tf_op | source)
XLA Modules:
  0.0 370.2 jit_solution(17127599141371032583)
XLA Ops:
  0.7 1.1 pad_maximum_fusion.6
  1.8 2.1 collective-permute-start
  3.8 4.5 %collective-permute-start.1 = (f32[2,32,512]{2,1,0:T(8,128)S(1)}, f32[2,32,512]{2,1,0:T(8,128)S(1)}, u32[]{:S(2)}, u32[]{:S(2)}) collective-permute-start(f32[2,32,512]{2,1,0:T(8,128)S(1)} %get-tuple-element.357), channel_id=1, source_target_pairs={{4,0},{8,4},{12,8},{16,12},{20,16},{24,20},{28,24},{5,1},{9,5},{13... | collective-permute-start | bytes 393224 | tf_op jit(solution)/shard_map/ppermute | solution.py:26
  8.4 0.7 collective-permute-done
  9.1 1.8 collective-permute-done.1
  10.9 2.3 pad_maximum_fusion.4
  13.2 3.5 collective-permute-start.2
  16.7 2.4 collective-permute-start.3
  19.1 1.3 copy.20
  20.4 8.2 %collective-permute-done.2 = f32[2,448,32]{2,1,0:T(8,128)} collective-permute-done((f32[2,448,32]{2,1,0:T(8,128)}, f32[2,448,32]{2,1,0:T(8,128)}, u32[]{:S(2)}, u32[]{:S(2)}) %collective-permute-start.2) | collective-permute-done | bytes 114720 | tf_op jit(solution)/shard_map/ppermute | solution.py:24
  28.6 3.2 collective-permute-done.3
  31.9 3.4 pad_maximum_fusion
  35.3 2.0 broadcast_in_dim.11
  37.2 75.7 %while.18 = (s32[]{:T(128)}, f32[3,448,576]{2,1,0:T(8,128)}, s32[]{:T(128)}, s32[8,2]{0,1:T(2,128)S(1)}, f32[2,448,576]{2,1,0:T(8,128)}, /*index=5*/f32[256,256]...) while((s32[]{:T(128)}, f32[3,448,576]{2,1,0:T(8,128)}, ...), condition=%wide.region_1.2_spmd.clone.clone, body=%wide.region_0.1_spmd.clone.clone.sunk | while | flops 2432040960 | bytes 17170828 | solution.py:109
  37.9 0.6 dynamic_slice.63
  40.4 0.6 constant_dynamic-slice_fusion.3
  43.6 1.3 multiply_subtract_fusion.2
  45.0 1.4 fusion.177
  46.3 1.4 fusion.178
  47.7 1.5 fusion.179
  49.2 1.5 convolution_bitcast_fusion.11
  50.7 1.5 convolution_bitcast_fusion.10
  52.1 2.6 fusion.180
  54.8 1.5 fusion.181
  56.3 1.5 fusion.182
  57.7 1.6 fusion.183
  59.3 1.7 convolution_bitcast_fusion.13
  61.0 1.4 convolution_bitcast_fusion.12
  62.4 1.5 add_bitcast_fusion.2
  63.9 1.6 maximum_add_fusion.2
  65.5 9.3 %dynamic_update_slice.9 = f32[3,448,576]{2,1,0:T(8,128)} dynamic-update-slice(f32[3,448,576]{2,1,0:T(8,128)} %get-tuple-element.454, f32[3,256,256]{2,1,0:T(8,128)S(1)} %maximum_add_fusion.2, s32[]{:T(128)} %constant.174.clone.1..sunk, s32[]{:T(128)S(6)} %select_n.173, s32[]{:T(128)S(6)} %select_n.174) | dynamic-update-slice | bytes 1572868 | tf_op jit(solution)/shard_map/while/body/dynamic_update_slice | solution.py:87
  78.0 0.6 constant_dynamic-slice_fusion.3
  81.2 1.3 multiply_subtract_fusion.2
  82.5 1.4 fusion.177
  83.9 1.4 fusion.178
  85.3 1.5 fusion.179
  86.7 1.5 convolution_bitcast_fusion.11
  88.2 1.5 convolution_bitcast_fusion.10
  89.7 2.6 fusion.180
  92.3 1.5 fusion.181
  93.8 1.5 fusion.182
  95.3 1.6 fusion.183
  96.9 1.7 convolution_bitcast_fusion.13
  98.5 1.4 convolution_bitcast_fusion.12
  99.9 1.5 add_bitcast_fusion.2
  101.5 1.6 maximum_add_fusion.2
  103.1 9.0 %dynamic_update_slice.9 = f32[3,448,576]{2,1,0:T(8,128)} dynamic-update-slice(f32[3,448,576]{2,1,0:T(8,128)} %get-tuple-element.454, f32[3,256,256]{2,1,0:T(8,128)S(1)} %maximum_add_fusion.2, s32[]{:T(128)} %constant.174.clone.1..sunk, s32[]{:T(128)S(6)} %select_n.173, s32[]{:T(128)S(6)} %select_n.174) | dynamic-update-slice | bytes 1572868 | tf_op jit(solution)/shard_map/while/body/dynamic_update_slice | solution.py:87
  112.9 1.1 fusion.123
  114.0 76.9 %collective-permute-start.4 = (f32[3,32,576]{2,1,0:T(8,128)S(1)}, f32[3,32,576]{2,1,0:T(8,128)S(1)}, u32[]{:S(2)}, u32[]{:S(2)}) collective-permute-start(f32[3,32,576]{2,1,0:T(8,128)S(1)} %get-tuple-element.351), channel_id=1, source_target_pairs={{4,0},{8,4},{12,8},{16,12},{20,16},{24,20},{28,24},{5,1},{9,5},{13... | collective-permute-start | bytes 663560 | tf_op jit(solution)/shard_map/ppermute | solution.py:36
  190.9 1.9 collective-permute-start.5
  192.9 1.8 collective-permute-done.4
  194.6 1.7 add_dynamic-update-slice_fusion
  196.3 110.9 %collective-permute-done.5 = f32[3,32,576]{2,1,0:T(8,128)S(1)} collective-permute-done((f32[3,32,576]{2,1,0:T(8,128)S(1)}, f32[3,32,576]{2,1,0:T(8,128)S(1)}, u32[]{:S(2)}, u32[]{:S(2)}) %collective-permute-start.5) | collective-permute-done | bytes 221216 | tf_op jit(solution)/shard_map/ppermute | solution.py:36
  307.2 1.7 fusion.121
  308.9 1.5 fusion.122
  310.6 1.9 collective-permute-start.6
  312.5 3.7 slice.174
  316.3 3.9 %collective-permute-start.7 = (f32[3,384,32]{1,2,0:T(8,128)S(1)}, f32[3,384,32]{1,2,0:T(8,128)S(1)}, u32[]{:S(2)}, u32[]{:S(2)}) collective-permute-start(f32[3,384,32]{1,2,0:T(8,128)S(1)} %copy.23), channel_id=1, source_target_pairs={{0,1},{1,2},{2,3},{4,5},{5,6},{6,7},{8,9},{9,10},{10,11},{12,13},{... | collective-permute-start | bytes 442376 | tf_op jit(solution)/shard_map/ppermute | solution.py:36
  320.5 1.2 slice_add_fusion.2
  321.7 3.3 scatter-add.16
  324.9 35.6 %collective-permute-done.7 = f32[3,384,32]{1,2,0:T(8,128)S(1)} collective-permute-done((f32[3,384,32]{1,2,0:T(8,128)S(1)}, f32[3,384,32]{1,2,0:T(8,128)S(1)}, u32[]{:S(2)}, u32[]{:S(2)}) %collective-permute-start.7) | collective-permute-done | bytes 147488 | tf_op jit(solution)/shard_map/ppermute | solution.py:36
  360.8 1.3 slice_add_fusion.1
  362.1 4.5 %scatter-add.19 = f32[3,384,576]{2,1,0:T(8,128)} dynamic-update-slice(f32[3,384,576]{2,1,0:T(8,128)} %scatter-add.16, f32[3,384,32]{2,1,0:T(8,128)S(1)} %slice_add_fusion.1, s32[]{:T(128)} %constant.174.clone.1, s32[]{:T(128)} %constant.174.clone.1, s32[]{:T(128)} %constant.181.clone.1) | dynamic-update-slice | bytes 294916 | tf_op jit(solution)/shard_map/scatter-add | solution.py:118
  366.6 3.6 fusion.118
  (23 shorter events, 1.5 us)
Async XLA Ops:
  0.6 18.4 %copy-start.1 = (f32[256,256]{1,0:T(8,128)S(1)}, f32[256,256]{1,0:T(8,128)}, u32[]{:S(2)}) copy-start(f32[256,256]{1,0:T(8,128)} %param.21) | copy-start | bytes 786436
  0.6 18.4 %copy-start = (f32[256,256]{1,0:T(8,128)S(1)}, f32[256,256]{1,0:T(8,128)}, u32[]{:S(2)}) copy-start(f32[256,256]{1,0:T(8,128)} %param.20) | copy-start | bytes 786436
  0.7 18.5 %copy-start.4 = (bf16[1,1,8,256,256]{4,3,2,1,0:T(8,128)(2,1)S(1)}, bf16[1,1,8,256,256]{4,3,2,1,0:T(8,128)(2,1)}, u32[]{:S(2)}) copy-start(bf16[1,1,8,256,256]{4,3,2,1,0:T(8,128)(2,1)} %param.22) | copy-start | bytes 3145732
  1.7 30.1 %copy-start.2 = (f32[384,512]{1,0:T(8,128)S(1)}, f32[384,512]{1,0:T(8,128)}, u32[]{:S(2)}) copy-start(f32[384,512]{1,0:T(8,128)} %param.19) | copy-start | bytes 2359300
  1.7 30.1 %copy-start.3 = (f32[384,512]{1,0:T(8,128)S(1)}, f32[384,512]{1,0:T(8,128)}, u32[]{:S(2)}) copy-start(f32[384,512]{1,0:T(8,128)} %param.18) | copy-start | bytes 2359300
  1.8 7.3 %collective-permute-start = (f32[2,32,512]{2,1,0:T(8,128)S(1)}, f32[2,32,512]{2,1,0:T(8,128)S(1)}, u32[]{:S(2)}, u32[]{:S(2)}) collective-permute-start(f32[2,32,512]{2,1,0:T(8,128)S(1)} %get-tuple-element.356), channel_id=1, source_target_pairs={{0,4},{4,8},{8,12},{12,16},{16,20},{20,24},{24,28},{1,5},{5,9},{9,... | collective-permute-start | bytes 393224 | tf_op jit(solution)/shard_map/ppermute | solution.py:24
  3.8 7.0 %collective-permute-start.1 = (f32[2,32,512]{2,1,0:T(8,128)S(1)}, f32[2,32,512]{2,1,0:T(8,128)S(1)}, u32[]{:S(2)}, u32[]{:S(2)}) collective-permute-start(f32[2,32,512]{2,1,0:T(8,128)S(1)} %get-tuple-element.357), channel_id=1, source_target_pairs={{4,0},{8,4},{12,8},{16,12},{20,16},{24,20},{28,24},{5,1},{9,5},{13... | collective-permute-start | bytes 393224 | tf_op jit(solution)/shard_map/ppermute | solution.py:26
  10.9 5.8 %copy-start.5 = (f32[2,32,512]{2,1,0:T(8,128)}, f32[2,32,512]{2,1,0:T(8,128)S(1)}, u32[]{:S(2)}) copy-start(f32[2,32,512]{2,1,0:T(8,128)S(1)} %collective-permute-done.1) | copy-start | bytes 393220
  13.2 15.5 %collective-permute-start.2 = (f32[2,448,32]{2,1,0:T(8,128)}, f32[2,448,32]{2,1,0:T(8,128)}, u32[]{:S(2)}, u32[]{:S(2)}) collective-permute-start(f32[2,448,32]{2,1,0:T(8,128)} %get-tuple-element.354), channel_id=1, source_target_pairs={{0,1},{1,2},{2,3},{4,5},{5,6},{6,7},{8,9},{9,10},{10,11},{12,13},{... | collective-permute-start | bytes 344072 | tf_op jit(solution)/shard_map/ppermute | solution.py:24
  16.7 15.2 %collective-permute-start.3 = (f32[2,448,32]{2,1,0:T(8,128)}, f32[2,448,32]{2,1,0:T(8,128)}, u32[]{:S(2)}, u32[]{:S(2)}) collective-permute-start(f32[2,448,32]{2,1,0:T(8,128)} %get-tuple-element.355), channel_id=1, source_target_pairs={{1,0},{2,1},{3,2},{5,4},{6,5},{7,6},{9,8},{10,9},{11,10},{13,12},{... | collective-permute-start | bytes 344072 | tf_op jit(solution)/shard_map/ppermute | solution.py:26
  35.3 2.0 copy-start.6
  35.3 2.0 copy-start.7
  114.0 80.6 %collective-permute-start.4 = (f32[3,32,576]{2,1,0:T(8,128)S(1)}, f32[3,32,576]{2,1,0:T(8,128)S(1)}, u32[]{:S(2)}, u32[]{:S(2)}) collective-permute-start(f32[3,32,576]{2,1,0:T(8,128)S(1)} %get-tuple-element.351), channel_id=1, source_target_pairs={{4,0},{8,4},{12,8},{16,12},{20,16},{24,20},{28,24},{5,1},{9,5},{13... | collective-permute-start | bytes 663560 | tf_op jit(solution)/shard_map/ppermute | solution.py:36
  190.9 116.3 %collective-permute-start.5 = (f32[3,32,576]{2,1,0:T(8,128)S(1)}, f32[3,32,576]{2,1,0:T(8,128)S(1)}, u32[]{:S(2)}, u32[]{:S(2)}) collective-permute-start(f32[3,32,576]{2,1,0:T(8,128)S(1)} %get-tuple-element.350), channel_id=1, source_target_pairs={{0,4},{4,8},{8,12},{12,16},{16,20},{20,24},{24,28},{1,5},{5,9},{9,... | collective-permute-start | bytes 663560 | tf_op jit(solution)/shard_map/ppermute | solution.py:36
  310.6 9.7 %collective-permute-start.6 = (f32[3,384,32]{1,2,0:T(8,128)S(1)}, f32[3,384,32]{1,2,0:T(8,128)S(1)}, u32[]{:S(2)}, u32[]{:S(2)}) collective-permute-start(f32[3,384,32]{1,2,0:T(8,128)S(1)} %copy.21), channel_id=1, source_target_pairs={{1,0},{2,1},{3,2},{5,4},{6,5},{7,6},{9,8},{10,9},{11,10},{13,12},{... | collective-permute-start | bytes 442376 | tf_op jit(solution)/shard_map/ppermute | solution.py:36
  316.3 44.2 %collective-permute-start.7 = (f32[3,384,32]{1,2,0:T(8,128)S(1)}, f32[3,384,32]{1,2,0:T(8,128)S(1)}, u32[]{:S(2)}, u32[]{:S(2)}) collective-permute-start(f32[3,384,32]{1,2,0:T(8,128)S(1)} %copy.23), channel_id=1, source_target_pairs={{0,1},{1,2},{2,3},{4,5},{5,6},{6,7},{8,9},{9,10},{10,11},{12,13},{... | collective-permute-start | bytes 442376 | tf_op jit(solution)/shard_map/ppermute | solution.py:36
where the time goes:
time: 375 us; the launch traced here: 370 us
  waiting for transfers between devices  162 us (43%)
  starting transfers between devices  97.1 us (26%)
  local copies, waits for them, and re-layouts  38.9 us (10%)
  matrix products  37.7 us (10%)
  other arithmetic  22.1 us (6%)
  loops' own time  11.5 us (3%)
    ppermute x4, waiting for transfers between devices, passed_along(): return lax.ppermute(shard, axis, pairs)  148 us
    ppermute x4, starting transfers between devices, passed_along(): return lax.ppermute(shard, axis, pairs)  84.7 us
    dynamic_update_slice x2, local copies, waits for them, and re-layouts, add_window(): return lax.dynamic_update_slice(acc, current + full, start)  18.3 us
    dot_general x8, matrix products, complex_dot(): jnp.dot(left_re + left_im, right_re + right_im, precision=highest, prefer...  14.4 us
    dot_general x8, matrix products, complex_dot(): jnp.dot(left_im, right_im, precision=highest, preferred_element_type=jnp....  12 us
    another operation x1, loops' own time, shards(): acc = lax.fori_loop(0, count, own_step, acc)  11.5 us
    dot_general x8, matrix products, complex_dot(): jnp.dot(left_re, right_re, precision=highest, preferred_element_type=jnp....  11.4 us
    ppermute x2, waiting for transfers between devices, padded_2(): lax.ppermute(tail, axis, [(i, (i + 1) % count) for i in range(ends)])  8.92 us
  transfers between devices with their start and end apart: 8, of which 7 were waited for; matrix products, arithmetic and copies ran while one was open for 3% of the time, Pallas kernels for 0%

commit v1 on v0

v1 whole, which is shorter than its diff:
```python
import functools
import math

import jax
import jax.numpy as jnp
import ml_dtypes
import numpy as np
from jax import lax
from jax.experimental import pallas as pl
from jax.experimental.pallas import tpu as pltpu
from jax.sharding import PartitionSpec as P

P_SIZE = 256
HALF = P_SIZE // 2
HALO = 32
LANES = 128
GROUPS = LANES // HALO
PAIR = 2

floor_amp = 0.5
ridge = 1.0

VMEM = pl.BlockSpec(memory_space=pltpu.VMEM)
SMEM = pl.BlockSpec(memory_space=pltpu.SMEM)
ANY = pl.BlockSpec(memory_space=pl.ANY)
PARAMS = pltpu.CompilerParams(vmem_limit_bytes=48 * 1024 * 1024)


def transform_tables():
    index = np.arange(HALF)
    plain = []
    for parity in (0, 1):
        angle = 2.0 * math.pi / P_SIZE * (index[:, None] * (2 * index[None, :] + parity) % P_SIZE)
        cos, sin = np.cos(angle), np.sin(angle)
        plain.append(np.block([[cos, -sin], [sin, cos]]) / math.sqrt(P_SIZE))
    parts = []
    for table in plain + [t.T for t in plain]:
        high = table.astype(np.float32).astype(ml_dtypes.bfloat16)
        low = (table - high.astype(np.float64)).astype(np.float32).astype(ml_dtypes.bfloat16)
        parts += [high, low]
    order = np.concatenate([np.arange(0, P_SIZE, 2), np.arange(1, P_SIZE, 2)])
    sort = np.zeros((P_SIZE, P_SIZE), np.float32)
    sort[np.arange(P_SIZE), order] = 1.0
    parts += [sort.astype(ml_dtypes.bfloat16), sort.T.astype(ml_dtypes.bfloat16)]
    return np.stack(parts)


def lane_index(rows):
    return lax.broadcasted_iota(jnp.int32, (rows, LANES), 1)


def pack_lanes(ref, rows, first):
    lane = lane_index(rows)
    packed = None
    for g in range(GROUPS):
        part = ref[g * rows : (g + 1) * rows, :]
        if g:
            part = pltpu.roll(part, HALO * g, 1)
        low = (first + HALO * g) % LANES
        mine = (lane >= low) & (lane < low + HALO)
        packed = part if packed is None else jnp.where(mine, part, packed)
    return packed


def unpack_lanes(packed, group):
    return pltpu.roll(packed, LANES - HALO * group, 1) if group else packed


def split(x):
    high = x.astype(jnp.bfloat16)
    return high, (x - high.astype(jnp.float32)).astype(jnp.bfloat16)


def product(left, right):
    return jnp.dot(left, right, preferred_element_type=jnp.float32)


def times_table(x, table, which):
    high, low = split(x)
    t_high, t_low = table[2 * which], table[2 * which + 1]
    return product(high, t_high) + (product(high, t_low) + product(low, t_high))


def table_times(table, which, x):
    high, low = split(x)
    t_high, t_low = table[2 * which], table[2 * which + 1]
    return product(t_high, high) + (product(t_low, high) + product(t_high, low))


def beside(*blocks):
    return jnp.concatenate(blocks, axis=1)


def below(*blocks):
    return jnp.concatenate(blocks, axis=0)


def ends(x):
    return x[:, :HALF], x[:, HALF:]


def forward_columns(exit_re, exit_im, table):
    re_lo, re_hi = ends(exit_re)
    im_lo, im_hi = ends(exit_im)
    even = times_table(beside(re_lo + re_hi, im_lo + im_hi), table, 0)
    odd = times_table(beside(re_lo - re_hi, im_lo - im_hi), table, 1)
    return even, odd


def forward_rows(even, odd, table):
    out = []
    for parity in (0, 1):
        if parity == 0:
            se, so = even[:HALF] + even[HALF:], odd[:HALF] + odd[HALF:]
        else:
            se, so = even[:HALF] - even[HALF:], odd[:HALF] - odd[HALF:]
        e_re, e_im = ends(se)
        o_re, o_im = ends(so)
        out.append(table_times(table, 2 + parity, below(beside(e_re, o_re), beside(e_im, o_im))))
    return out


def residual(far, frame):
    out = []
    for parity in (0, 1):
        re, im = far[parity][:HALF], far[parity][HALF:]
        level = jnp.maximum(re * re + im * im, floor_amp * floor_amp)
        inten = frame[parity * HALF : (parity + 1) * HALF]
        factor = 1.0 - inten * lax.rsqrt(inten * level)
        out.append(below(re * factor, im * factor))
    return out


def back_rows(res, table):
    first = table_times(table, 0, res[0])
    second = table_times(table, 1, res[1])
    upper, lower = first + second, first - second
    out = []
    for cols in (slice(0, HALF), slice(HALF, P_SIZE)):
        out.append(
            below(
                beside(upper[:HALF, cols], upper[HALF:, cols]),
                beside(lower[:HALF, cols], lower[HALF:, cols]),
            )
        )
    return out


def back_columns(parts, table):
    even = times_table(parts[0], table, 2)
    odd = times_table(parts[1], table, 3)
    lo, hi = even + odd, even - odd
    return beside(lo[:, :HALF], hi[:, :HALF]), beside(lo[:, HALF:], hi[:, HALF:])


def window_kernel(
    counts, offsets, chosen, obj_re, obj_im, above, under, left, right,
    probe_re, probe_im, frames, table,
    acc_out, to_left, to_right,
    cells, acc, strip, sems,
):
    tile_r, tile_c = obj_re.shape
    rows = tile_r + 2 * HALO
    layers = acc.shape[0]
    inner = slice(HALO, HALO + tile_r)
    middle = slice(LANES, LANES + tile_c)
    copies = []
    for k, ref in enumerate((obj_re, obj_im)):
        copies.append(pltpu.make_async_copy(ref, cells.at[k, inner, middle], sems.at[3 * k]))
        copies.append(pltpu.make_async_copy(above.at[k], cells.at[k, 0:HALO, middle], sems.at[3 * k + 1]))
        copies.append(
            pltpu.make_async_copy(under.at[k], cells.at[k, rows - HALO : rows, middle], sems.at[3 * k + 2])
        )
    for copy in copies:
        copy.start()
    group_rows = 2 * rows // GROUPS
    for g in range(GROUPS):
        k, start = divmod(g * group_rows, rows)
        piece = slice(start, start + group_rows)
        cells[k, piece, 0:LANES] = unpack_lanes(left[...], g)
        cells[k, piece, LANES + tile_c :] = unpack_lanes(right[...], g)
    acc[...] = jnp.zeros_like(acc)
    for copy in copies:
        copy.wait()

    count = counts[0, 0]
    lane = lane_index(P_SIZE)

    def load(slot):
        row = pl.multiple_of(offsets[0, 0, slot, 0] + HALO, 16)
        col = offsets[0, 0, slot, 1] + LANES
        turn = lax.rem(col, LANES)
        base = pl.multiple_of(col - turn, LANES)
        keep = lane >= turn
        w_re = pltpu.roll(probe_re[...], turn, 1)
        w_im = pltpu.roll(probe_im[...], turn, 1)
        patch = []
        for k in (0, 1):
            block = cells[k, pl.ds(row, P_SIZE), pl.ds(base, 3 * LANES)]
            patch.append(
                beside(jnp.where(keep, block[:, :LANES], block[:, 2 * LANES :]), block[:, LANES : 2 * LANES])
            )
        exit_re = w_re * patch[0] - w_im * patch[1]
        exit_im = w_re * patch[1] + w_im * patch[0]
        return (row, base, keep, w_re, w_im), exit_re, exit_im

    def frame_of(slot):
        sort, unsort = table[8], table[9]
        half = product(sort, frames[chosen[0, 0, slot]]).astype(jnp.bfloat16)
        return product(half, unsort)

    def place(where, back_re, back_im):
        row, base, keep, w_re, w_im = where
        terms = (
            w_re * back_re + w_im * back_im,
            w_re * back_im - w_im * back_re,
            w_re * w_re + w_im * w_im,
        )
        for k in range(layers):
            lo, hi = ends(terms[k])
            parts = (jnp.where(keep, lo, 0.0), hi, jnp.where(keep, 0.0, lo))
            for t, part in enumerate(parts):
                acc[k, pl.ds(row, P_SIZE), pl.ds(base + t * LANES, LANES)] += part

    def step(pair, carry):
        slots = [jnp.minimum(pair * PAIR + i, count - 1) for i in range(PAIR)]
        frame = [frame_of(slot) for slot in slots]
        loaded = [load(slot) for slot in slots]
        state = [forward_columns(x[1], x[2], table) for x in loaded]
        state = [forward_rows(*x, table) for x in state]
        state = [residual(x, f) for x, f in zip(state, frame)]
        state = [back_rows(x, table) for x in state]
        state = [back_columns(x, table) for x in state]
        place(loaded[0][0], *state[0])
        for i in range(1, PAIR):
            pl.when(pair * PAIR + i < count)(functools.partial(place, loaded[i][0], *state[i]))
        return carry

    lax.fori_loop(0, (count + PAIR - 1) // PAIR, step, 0)

    out = pltpu.make_async_copy(acc.at[:, :, middle], acc_out, sems.at[0])
    out.start()
    group_rows = layers * rows // GROUPS
    for tile, first, dest in ((0, LANES - HALO, to_left), (LANES + tile_c, 0, to_right)):
        for k in range(layers):
            strip[k * rows : (k + 1) * rows, :] = acc[k, :, tile : tile + LANES]
        dest[...] = pack_lanes(strip, group_rows, first)
    out.wait()


def column_strips(obj_re, obj_im, above, under, to_left, to_right, strip, sems):
    tile_r, tile_c = obj_re.shape
    rows = tile_r + 2 * HALO
    copies = []
    for side, start in ((0, 0), (1, tile_c - LANES)):
        cols = slice(start, start + LANES)
        for k, ref in enumerate((obj_re, obj_im)):
            top = k * rows
            base = 6 * side + 3 * k
            copies += [
                pltpu.make_async_copy(above.at[k, :, cols], strip.at[side, top : top + HALO], sems.at[base]),
                pltpu.make_async_copy(
                    ref.at[:, cols], strip.at[side, top + HALO : top + HALO + tile_r], sems.at[base + 1]
                ),
                pltpu.make_async_copy(
                    under.at[k, :, cols], strip.at[side, top + rows - HALO : top + rows], sems.at[base + 2]
                ),
            ]
    for copy in copies:
        copy.start()
    for copy in copies:
        copy.wait()
    group_rows = 2 * rows // GROUPS
    to_left[...] = pack_lanes(strip.at[0], group_rows, 0)
    to_right[...] = pack_lanes(strip.at[1], group_rows, LANES - HALO)


def add_side_strips(add, packed, layers, rows, first):
    group_rows = layers * rows // GROUPS
    lane = lane_index(group_rows)
    mine = (lane >= first) & (lane < first + HALO)
    for g in range(GROUPS):
        part = jnp.where(mine, unpack_lanes(packed, g), 0.0)
        done = 0
        while done < group_rows:
            layer, row = divmod(g * group_rows + done, rows)
            size = min(group_rows - done, rows - row)
            add(layer, row, part[done : done + size])
            done += size


def row_strips(acc, from_left, from_right, up, down, whole):
    layers, rows, width = acc.shape
    whole[...] = acc[...]
    for packed, first, col in ((from_left, 0, 0), (from_right, LANES - HALO, width - LANES)):

        def add(layer, row, part):
            whole[layer, row : row + part.shape[0], col : col + LANES] += part

        add_side_strips(add, packed[...], layers, rows, first)
    up[...] = whole[:, 0:HALO, :]
    down[...] = whole[:, rows - HALO : rows, :]


def finish(whole, from_above, from_under, obj_re, obj_im, new_re, new_im):
    layers, rows, width = whole.shape
    tile_r = rows - 2 * HALO
    for start, size, extra in (
        (0, HALO, from_above),
        (HALO, tile_r - 2 * HALO, None),
        (tile_r - HALO, HALO, from_under),
    ):
        part = [whole[k, HALO + start : HALO + start + size, :] for k in range(layers)]
        if extra is not None:
            part = [part[k] + extra[k] for k in range(layers)]
        scale = 1.0 / (part[2] + ridge)
        new_re[start : start + size, :] = obj_re[start : start + size, :] - part[0] * scale
        new_im[start : start + size, :] = obj_im[start : start + size, :] - part[1] * scale


def passed_along(shard, axis, by):
    devices = lax.axis_size(axis)
    pairs = [(i, i + by) for i in range(devices) if 0 <= i + by < devices]
    return lax.ppermute(shard, axis, pairs)


def f32(*shape):
    return jax.ShapeDtypeStruct(shape, jnp.float32)


def shards(object_re, object_im, probe_re, probe_im, frames, counts, offsets, frame_index):
    tile_r, tile_c = object_re.shape
    rows = tile_r + 2 * HALO
    layers = 3
    table = jnp.asarray(transform_tables())

    stacked_top = jnp.stack([object_re[:HALO], object_im[:HALO]])
    stacked_end = jnp.stack([object_re[tile_r - HALO :], object_im[tile_r - HALO :]])
    above = passed_along(stacked_end, "row", 1)
    under = passed_along(stacked_top, "row", -1)

    strip_rows = 2 * rows // GROUPS
    to_left, to_right = pl.pallas_call(
        column_strips,
        out_shape=(f32(strip_rows, LANES), f32(strip_rows, LANES)),
        in_specs=[ANY] * 4,
        out_specs=(VMEM, VMEM),
        scratch_shapes=[pltpu.VMEM((2, 2 * rows, LANES), jnp.float32), pltpu.SemaphoreType.DMA((12,))],
        compiler_params=PARAMS,
        name="column_strips",
    )(object_re, object_im, above, under)
    left = passed_along(to_right, "col", 1)
    right = passed_along(to_left, "col", -1)

    spill_rows = layers * rows // GROUPS
    acc, to_left, to_right = pl.pallas_call(
        window_kernel,
        out_shape=(f32(layers, rows, tile_c), f32(spill_rows, LANES), f32(spill_rows, LANES)),
        in_specs=[SMEM] * 3 + [ANY] * 4 + [VMEM] * 6,
        out_specs=(ANY, VMEM, VMEM),
        scratch_shapes=[
            pltpu.VMEM((2, rows, tile_c + 2 * LANES), jnp.float32),
            pltpu.VMEM((layers, rows, tile_c + 2 * LANES), jnp.float32),
            pltpu.VMEM((layers * rows, LANES), jnp.float32),
            pltpu.SemaphoreType.DMA((6,)),
        ],
        compiler_params=PARAMS,
        name="windows",
    )(
        counts, offsets, frame_index, object_re, object_im, above, under, left, right,
        probe_re, probe_im, frames.reshape(frames.shape[2:]), table,
    )
    from_right = passed_along(to_left, "col", -1)
    from_left = passed_along(to_right, "col", 1)

    up, down, whole = pl.pallas_call(
        row_strips,
        out_shape=(f32(layers, HALO, tile_c), f32(layers, HALO, tile_c), f32(layers, rows, tile_c)),
        in_specs=[VMEM] * 3,
        out_specs=(VMEM,) * 3,
        compiler_params=PARAMS,
        name="row_strips",
    )(acc, from_left, from_right)
    from_under = passed_along(up, "row", -1)
    from_above = passed_along(down, "row", 1)

    return pl.pallas_call(
        finish,
        out_shape=(f32(tile_r, tile_c), f32(tile_r, tile_c)),
        in_specs=[VMEM] * 5,
        out_specs=(VMEM, VMEM),
        compiler_params=PARAMS,
        name="finish",
    )(whole, from_above, from_under, object_re, object_im)


def solution(mesh):
    return jax.shard_map(
        shards,
        mesh=mesh,
        in_specs=(
            P("row", "col"),
            P("row", "col"),
            P(),
            P(),
            P("row", "col", None, None, None),
            P("row", "col"),
            P("row", "col", None, None),
            P("row", "col", None),
        ),
        out_specs=(P("row", "col"), P("row", "col")),
        check_vma=False,
    )
```

time: 375 us -> 68 us (0.18)
  the two profiles are of different devices: /device:TPU:20 before, /device:TPU:3 now
where the time goes in v1:
time: 68 us; the launch traced here: 67.5 us
  starting transfers between devices  25.9 us (38%)
  waiting for transfers between devices  22.1 us (32%)
  Pallas kernels  9.95 us (15%)
  local copies, waits for them, and re-layouts  8.03 us (12%)
  between operations  1.46 us (2%)
    ppermute x8, starting transfers between devices, passed_along(): return lax.ppermute(shard, axis, pairs)  25.9 us
    ppermute x8, waiting for transfers between devices, passed_along(): return lax.ppermute(shard, axis, pairs)  22.1 us
    unnamed x23, local copies, waits for them, and re-layouts  6.99 us
    pallas_call x1, Pallas kernels, shards(): pl.pallas_call(window_kernel, out_shape=(f32(layers, rows, tile_c), f32(s...  5.85 us
    pallas_call x1, Pallas kernels, shards(): pl.pallas_call(row_strips, out_shape=(f32(layers, HALO, tile_c), f32(laye...  2.21 us
    pallas_call x1, Pallas kernels, shards(): pl.pallas_call(finish, out_shape=(f32(tile_r, tile_c), f32(tile_r, tile_c...  1.37 us
  transfers between devices with their start and end apart: 8, of which 6 were waited for; matrix products, arithmetic and copies ran while one was open for 0% of the time, Pallas kernels for 0%

profile of v1, /device:TPU:3, one launch (start us, length us, event | category | flops | bytes accessed | tf_op | source)
XLA Modules:
  0.0 67.5 jit_solution(15465393367421858403)
XLA Ops:
  0.6 0.0 copy-start.1
  0.6 0.0 copy-start.10
  0.7 0.0 copy-start.9
  0.7 0.0 copy-start.7
  0.7 1.0 %slice_bitcast_fusion = (f32[1,32,512]{2,1,0:T(8,128)S(1)}, f32[1,32,512]{2,1,0:T(8,128)S(1)}, f32[1,32,512]{2,1,0:T(8,128)S(1)}, f32[1,32,512]{2,1,0:T(8,128)S(1)}) fusion(f32[384,512]{1,0:T(8,128)} %obj_im.5, f32[384,512]{1,0:T(8,128)} %obj_re.5), kind=kLoop, calls=%fused_computation.2 | loop fusion | bytes 524288 | tf_op jit(solution)/shard_map/stack | solution.py:337
  1.7 3.7 %collective-permute-start = (f32[2,32,512]{2,1,0:T(8,128)S(1)}, f32[2,32,512]{2,1,0:T(8,128)S(1)}, u32[]{:S(2)}, u32[]{:S(2)}) collective-permute-start(f32[2,32,512]{2,1,0:T(8,128)S(1)} %pad_maximum_fusion), channel_id=1, source_target_pairs={{0,4},{4,8},{8,12},{12,16},{16,20},{20,24},{24,28},{1,5},{5,9},{9,... | collective-permute-start | bytes 393224 | tf_op jit(solution)/shard_map/ppermute | solution.py:324
  5.4 1.9 %collective-permute-start.1 = (f32[2,32,512]{2,1,0:T(8,128)S(1)}, f32[2,32,512]{2,1,0:T(8,128)S(1)}, u32[]{:S(2)}, u32[]{:S(2)}) collective-permute-start(f32[2,32,512]{2,1,0:T(8,128)S(1)} %pad_maximum_fusion.1), channel_id=1, source_target_pairs={{4,0},{8,4},{12,8},{16,12},{20,16},{24,20},{28,24},{5,1},{9,5},{13... | collective-permute-start | bytes 393224 | tf_op jit(solution)/shard_map/ppermute | solution.py:324
  7.4 0.0 collective-permute-done.above
  7.4 5.2 %collective-permute-done.1.under = f32[2,32,512]{2,1,0:T(8,128)S(1)} collective-permute-done((f32[2,32,512]{2,1,0:T(8,128)S(1)}, f32[2,32,512]{2,1,0:T(8,128)S(1)}, u32[]{:S(2)}, u32[]{:S(2)}) %collective-permute-start.1) | collective-permute-done | bytes 131104 | tf_op jit(solution)/shard_map/ppermute | solution.py:324
  12.6 0.0 copy-start
  12.6 1.1 %copy-done = f32[384,512]{1,0:T(8,128)S(1)} copy-done((f32[384,512]{1,0:T(8,128)S(1)}, f32[384,512]{1,0:T(8,128)}, u32[]{:S(2)}) %copy-start) | copy-done | bytes 786456
  13.8 0.0 copy-start.2
  13.8 1.1 %copy-done.2 = f32[384,512]{1,0:T(8,128)S(1)} copy-done((f32[384,512]{1,0:T(8,128)S(1)}, f32[384,512]{1,0:T(8,128)}, u32[]{:S(2)}) %copy-start.2) | copy-done | bytes 786456
  14.9 0.5 column_strips.1
  15.4 3.2 %collective-permute-start.2 = (f32[224,128]{1,0:T(8,128)S(1)}, f32[224,128]{1,0:T(8,128)S(1)}, u32[]{:S(2)}, u32[]{:S(2)}) collective-permute-start(f32[224,128]{1,0:T(8,128)S(1)} %get-tuple-element.10), channel_id=1, source_target_pairs={{0,1},{1,2},{2,3},{4,5},{5,6},{6,7},{8,9},{9,10},{10,11},{12,13},{... | collective-permute-start | bytes 344072 | tf_op jit(solution)/shard_map/ppermute | solution.py:324
  18.6 1.3 %collective-permute-start.3 = (f32[224,128]{1,0:T(8,128)S(1)}, f32[224,128]{1,0:T(8,128)S(1)}, u32[]{:S(2)}, u32[]{:S(2)}) collective-permute-start(f32[224,128]{1,0:T(8,128)S(1)} %get-tuple-element.11), channel_id=1, source_target_pairs={{1,0},{2,1},{3,2},{5,4},{6,5},{7,6},{9,8},{10,9},{11,10},{13,12},{... | collective-permute-start | bytes 344072 | tf_op jit(solution)/shard_map/ppermute | solution.py:324
  20.6 0.0 copy-done.10
  20.6 0.1 copy.11.offsets
  20.7 0.0 collective-permute-done.2.left
  20.7 3.5 %collective-permute-done.3.right = f32[224,128]{1,0:T(8,128)S(1)} collective-permute-done((f32[224,128]{1,0:T(8,128)S(1)}, f32[224,128]{1,0:T(8,128)S(1)}, u32[]{:S(2)}, u32[]{:S(2)}) %collective-permute-start.3) | collective-permute-done | bytes 114720 | tf_op jit(solution)/shard_map/ppermute | solution.py:324
  24.2 0.0 copy-done.1
  24.2 0.0 copy-done.9
  24.2 0.0 copy-done.7
  24.2 0.0 copy-start.3
  24.2 1.1 %copy-done.3 = f32[384,512]{1,0:T(8,128)S(1)} copy-done((f32[384,512]{1,0:T(8,128)S(1)}, f32[384,512]{1,0:T(8,128)}, u32[]{:S(2)}) %copy-start.3) | copy-done | bytes 786456
  25.3 0.0 copy-start.5
  25.3 1.3 %copy-done.5 = bf16[10,256,256]{2,1,0:T(8,128)(2,1)S(1)} copy-done((bf16[10,256,256]{2,1,0:T(8,128)(2,1)S(1)}, bf16[10,256,256]{2,1,0:T(8,128)(2,1)}, u32[]{:S(2)}) %copy-start.5) | copy-done | bytes 1310744
  26.6 0.0 copy-start.6
  26.6 1.2 %copy-done.6 = bf16[1,1,8,256,256]{4,3,2,1,0:T(8,128)(2,1)S(1)} copy-done((bf16[1,1,8,256,256]{4,3,2,1,0:T(8,128)(2,1)S(1)}, bf16[1,1,8,256,256]{4,3,2,1,0:T(8,128)(2,1)}, u32[]{:S(2)}) %copy-start.6) | copy-done | bytes 1048600
  27.9 0.0 copy-start.8
  27.9 0.9 %copy-done.8 = f32[256,256]{1,0:T(8,128)S(1)} copy-done((f32[256,256]{1,0:T(8,128)S(1)}, f32[256,256]{1,0:T(8,128)}, u32[]{:S(2)}) %copy-start.8) | copy-done | bytes 262168
  28.8 5.9 %windows.1 = (f32[3,448,512]{2,1,0:T(8,128)}, f32[336,128]{1,0:T(8,128)S(1)}, f32[336,128]{1,0:T(8,128)S(1)}) custom-call(s32[1,1]{1,0:T(1,128)S(6)} %copy.12.counts, s32[1,1,8,2]{3,2,1,0:T(8,128)S(1)} %copy.11.offsets, s32[1,1,8]{2,1,0:T(1,128)S(1)} %copy-done.9, f32[384,512]{1,0:T(8,128)S(1)} %copy-done.1, f32[384,512]{1,0:T(8,128)S(1)} %copy-done.3, ...), custom_call_target="tpu_custom_call" | custom-call | tf_op jit(solution)/shard_map/windows/pallas_call | solution.py:356
  34.7 0.0 copy-start.4
  34.7 3.1 %collective-permute-start.4 = (f32[336,128]{1,0:T(8,128)S(1)}, f32[336,128]{1,0:T(8,128)S(1)}, u32[]{:S(2)}, u32[]{:S(2)}) collective-permute-start(f32[336,128]{1,0:T(8,128)S(1)} %get-tuple-element.13), channel_id=1, source_target_pairs={{0,1},{1,2},{2,3},{4,5},{5,6},{6,7},{8,9},{9,10},{10,11},{12,13},{... | collective-permute-start | bytes 516104 | tf_op jit(solution)/shard_map/ppermute | solution.py:324
  37.7 1.3 %collective-permute-start.5 = (f32[336,128]{1,0:T(8,128)S(1)}, f32[336,128]{1,0:T(8,128)S(1)}, u32[]{:S(2)}, u32[]{:S(2)}) collective-permute-start(f32[336,128]{1,0:T(8,128)S(1)} %get-tuple-element.14), channel_id=1, source_target_pairs={{1,0},{2,1},{3,2},{5,4},{6,5},{7,6},{9,8},{10,9},{11,10},{13,12},{... | collective-permute-start | bytes 516104 | tf_op jit(solution)/shard_map/ppermute | solution.py:324
  39.0 2.6 %collective-permute-done.4.from_left = f32[336,128]{1,0:T(8,128)S(1)} collective-permute-done((f32[336,128]{1,0:T(8,128)S(1)}, f32[336,128]{1,0:T(8,128)S(1)}, u32[]{:S(2)}, u32[]{:S(2)}) %collective-permute-start.4) | collective-permute-done | bytes 172064 | tf_op jit(solution)/shard_map/ppermute | solution.py:324
  41.6 4.8 %collective-permute-done.5.from_right = f32[336,128]{1,0:T(8,128)S(1)} collective-permute-done((f32[336,128]{1,0:T(8,128)S(1)}, f32[336,128]{1,0:T(8,128)S(1)}, u32[]{:S(2)}, u32[]{:S(2)}) %collective-permute-start.5) | collective-permute-done | bytes 172064 | tf_op jit(solution)/shard_map/ppermute | solution.py:324
  46.5 2.2 %row_strips.1 = (f32[3,32,512]{2,1,0:T(8,128)S(1)}, f32[3,32,512]{2,1,0:T(8,128)S(1)}, f32[3,448,512]{2,1,0:T(8,128)S(1)}) custom-call(f32[3,448,512]{2,1,0:T(8,128)} %get-tuple-element.12.acc, f32[336,128]{1,0:T(8,128)S(1)} %collective-permute-done.4.from_left, f32[336,128]{1,0:T(8,128)S(1)} %collective-permute-done.5.from_right), custom_call_target="tpu_custom_call" | custom-call | tf_op jit(solution)/shard_map/row_strips/pallas_call | solution.py:376
  48.7 9.5 %collective-permute-start.6 = (f32[3,32,512]{2,1,0:T(8,128)S(1)}, f32[3,32,512]{2,1,0:T(8,128)S(1)}, u32[]{:S(2)}, u32[]{:S(2)}) collective-permute-start(f32[3,32,512]{2,1,0:T(8,128)S(1)} %get-tuple-element.16), channel_id=1, source_target_pairs={{0,4},{4,8},{8,12},{12,16},{16,20},{20,24},{24,28},{1,5},{5,9},{9,... | collective-permute-start | bytes 589832 | tf_op jit(solution)/shard_map/ppermute | solution.py:324
  58.3 1.9 %collective-permute-start.7 = (f32[3,32,512]{2,1,0:T(8,128)S(1)}, f32[3,32,512]{2,1,0:T(8,128)S(1)}, u32[]{:S(2)}, u32[]{:S(2)}) collective-permute-start(f32[3,32,512]{2,1,0:T(8,128)S(1)} %get-tuple-element.17), channel_id=1, source_target_pairs={{4,0},{8,4},{12,8},{16,12},{20,16},{24,20},{28,24},{5,1},{9,5},{13... | collective-permute-start | bytes 589832 | tf_op jit(solution)/shard_map/ppermute | solution.py:324
  60.2 2.2 %collective-permute-done.6.from_above = f32[3,32,512]{2,1,0:T(8,128)S(1)} collective-permute-done((f32[3,32,512]{2,1,0:T(8,128)S(1)}, f32[3,32,512]{2,1,0:T(8,128)S(1)}, u32[]{:S(2)}, u32[]{:S(2)}) %collective-permute-start.6) | collective-permute-done | bytes 196640 | tf_op jit(solution)/shard_map/ppermute | solution.py:324
  62.4 3.8 %collective-permute-done.7.from_under = f32[3,32,512]{2,1,0:T(8,128)S(1)} collective-permute-done((f32[3,32,512]{2,1,0:T(8,128)S(1)}, f32[3,32,512]{2,1,0:T(8,128)S(1)}, u32[]{:S(2)}, u32[]{:S(2)}) %collective-permute-start.7) | collective-permute-done | bytes 196640 | tf_op jit(solution)/shard_map/ppermute | solution.py:324
  66.1 0.0 copy-done.4
  66.1 1.4 %finish.1 = (f32[384,512]{1,0:T(8,128)}, f32[384,512]{1,0:T(8,128)}) custom-call(f32[3,448,512]{2,1,0:T(8,128)S(1)} %get-tuple-element.15.whole, f32[3,32,512]{2,1,0:T(8,128)S(1)} %collective-permute-done.6.from_above, f32[3,32,512]{2,1,0:T(8,128)S(1)} %collective-permute-done.7.from_under, f32[384,512]{1,0:T(8,128)S(1)} %copy-done.1, f32[384,512]{1,0:T(8,128)S(1)} %copy-done.4), custom_call_target="tpu_custom_call" | custom-call | tf_op jit(solution)/shard_map/finish/pallas_call | solution.py:387
  (2 shorter events, 0.0 us)
Async XLA Ops:
  0.6 23.5 %copy-start.1 = (f32[384,512]{1,0:T(8,128)S(1)}, f32[384,512]{1,0:T(8,128)}, u32[]{:S(2)}) copy-start(f32[384,512]{1,0:T(8,128)} %obj_re.5) | copy-start | bytes 2359300
  0.6 19.9 %copy-start.10 = (s32[1,1,8,2]{2,3,1,0:T(2,128)S(1)}, s32[1,1,8,2]{2,3,1,0:T(2,128)}, u32[]{:S(2)}) copy-start(s32[1,1,8,2]{2,3,1,0:T(2,128)} %param.15) | copy-start | bytes 196
  0.7 23.5 %copy-start.9 = (s32[1,1,8]{2,1,0:T(1,128)S(1)}, s32[1,1,8]{2,1,0:T(1,128)}, u32[]{:S(2)}) copy-start(s32[1,1,8]{2,1,0:T(1,128)} %chosen.1) | copy-start | bytes 100
  0.7 23.5 %copy-start.7 = (f32[256,256]{1,0:T(8,128)S(1)}, f32[256,256]{1,0:T(8,128)}, u32[]{:S(2)}) copy-start(f32[256,256]{1,0:T(8,128)} %probe_re.1) | copy-start | bytes 786436
  1.7 5.6 %collective-permute-start = (f32[2,32,512]{2,1,0:T(8,128)S(1)}, f32[2,32,512]{2,1,0:T(8,128)S(1)}, u32[]{:S(2)}, u32[]{:S(2)}) collective-permute-start(f32[2,32,512]{2,1,0:T(8,128)S(1)} %pad_maximum_fusion), channel_id=1, source_target_pairs={{0,4},{4,8},{8,12},{12,16},{16,20},{20,24},{24,28},{1,5},{5,9},{9,... | collective-permute-start | bytes 393224 | tf_op jit(solution)/shard_map/ppermute | solution.py:324
  5.4 7.2 %collective-permute-start.1 = (f32[2,32,512]{2,1,0:T(8,128)S(1)}, f32[2,32,512]{2,1,0:T(8,128)S(1)}, u32[]{:S(2)}, u32[]{:S(2)}) collective-permute-start(f32[2,32,512]{2,1,0:T(8,128)S(1)} %pad_maximum_fusion.1), channel_id=1, source_target_pairs={{4,0},{8,4},{12,8},{16,12},{20,16},{24,20},{28,24},{5,1},{9,5},{13... | collective-permute-start | bytes 393224 | tf_op jit(solution)/shard_map/ppermute | solution.py:324
  12.6 1.1 %copy-start = (f32[384,512]{1,0:T(8,128)S(1)}, f32[384,512]{1,0:T(8,128)}, u32[]{:S(2)}) copy-start(f32[384,512]{1,0:T(8,128)} %obj_re.5) | copy-start | bytes 2359300
  13.8 1.1 %copy-start.2 = (f32[384,512]{1,0:T(8,128)S(1)}, f32[384,512]{1,0:T(8,128)}, u32[]{:S(2)}) copy-start(f32[384,512]{1,0:T(8,128)} %obj_im.5) | copy-start | bytes 2359300
  15.4 5.3 %collective-permute-start.2 = (f32[224,128]{1,0:T(8,128)S(1)}, f32[224,128]{1,0:T(8,128)S(1)}, u32[]{:S(2)}, u32[]{:S(2)}) collective-permute-start(f32[224,128]{1,0:T(8,128)S(1)} %get-tuple-element.10), channel_id=1, source_target_pairs={{0,1},{1,2},{2,3},{4,5},{5,6},{6,7},{8,9},{9,10},{10,11},{12,13},{... | collective-permute-start | bytes 344072 | tf_op jit(solution)/shard_map/ppermute | solution.py:324
  18.6 5.5 %collective-permute-start.3 = (f32[224,128]{1,0:T(8,128)S(1)}, f32[224,128]{1,0:T(8,128)S(1)}, u32[]{:S(2)}, u32[]{:S(2)}) collective-permute-start(f32[224,128]{1,0:T(8,128)S(1)} %get-tuple-element.11), channel_id=1, source_target_pairs={{1,0},{2,1},{3,2},{5,4},{6,5},{7,6},{9,8},{10,9},{11,10},{13,12},{... | collective-permute-start | bytes 344072 | tf_op jit(solution)/shard_map/ppermute | solution.py:324
  24.2 1.1 %copy-start.3 = (f32[384,512]{1,0:T(8,128)S(1)}, f32[384,512]{1,0:T(8,128)}, u32[]{:S(2)}) copy-start(f32[384,512]{1,0:T(8,128)} %obj_im.5) | copy-start | bytes 2359300
  25.3 1.3 %copy-start.5 = (bf16[10,256,256]{2,1,0:T(8,128)(2,1)S(1)}, bf16[10,256,256]{2,1,0:T(8,128)(2,1)}, u32[]{:S(2)}) copy-start(bf16[10,256,256]{2,1,0:T(8,128)(2,1)} %constant.2.clone.table) | copy-start | bytes 3932164
  26.6 1.2 %copy-start.6 = (bf16[1,1,8,256,256]{4,3,2,1,0:T(8,128)(2,1)S(1)}, bf16[1,1,8,256,256]{4,3,2,1,0:T(8,128)(2,1)}, u32[]{:S(2)}) copy-start(bf16[1,1,8,256,256]{4,3,2,1,0:T(8,128)(2,1)} %param.13) | copy-start | bytes 3145732
  27.9 0.9 %copy-start.8 = (f32[256,256]{1,0:T(8,128)S(1)}, f32[256,256]{1,0:T(8,128)}, u32[]{:S(2)}) copy-start(f32[256,256]{1,0:T(8,128)} %probe_im.1) | copy-start | bytes 786436
  34.7 31.5 %copy-start.4 = (f32[384,512]{1,0:T(8,128)S(1)}, f32[384,512]{1,0:T(8,128)}, u32[]{:S(2)}) copy-start(f32[384,512]{1,0:T(8,128)} %obj_im.5) | copy-start | bytes 2359300
  34.7 7.0 %collective-permute-start.4 = (f32[336,128]{1,0:T(8,128)S(1)}, f32[336,128]{1,0:T(8,128)S(1)}, u32[]{:S(2)}, u32[]{:S(2)}) collective-permute-start(f32[336,128]{1,0:T(8,128)S(1)} %get-tuple-element.13), channel_id=1, source_target_pairs={{0,1},{1,2},{2,3},{4,5},{5,6},{6,7},{8,9},{9,10},{10,11},{12,13},{... | collective-permute-start | bytes 516104 | tf_op jit(solution)/shard_map/ppermute | solution.py:324
  37.7 8.7 %collective-permute-start.5 = (f32[336,128]{1,0:T(8,128)S(1)}, f32[336,128]{1,0:T(8,128)S(1)}, u32[]{:S(2)}, u32[]{:S(2)}) collective-permute-start(f32[336,128]{1,0:T(8,128)S(1)} %get-tuple-element.14), channel_id=1, source_target_pairs={{1,0},{2,1},{3,2},{5,4},{6,5},{7,6},{9,8},{10,9},{11,10},{13,12},{... | collective-permute-start | bytes 516104 | tf_op jit(solution)/shard_map/ppermute | solution.py:324
  48.7 13.7 %collective-permute-start.6 = (f32[3,32,512]{2,1,0:T(8,128)S(1)}, f32[3,32,512]{2,1,0:T(8,128)S(1)}, u32[]{:S(2)}, u32[]{:S(2)}) collective-permute-start(f32[3,32,512]{2,1,0:T(8,128)S(1)} %get-tuple-element.16), channel_id=1, source_target_pairs={{0,4},{4,8},{8,12},{12,16},{16,20},{20,24},{24,28},{1,5},{5,9},{9,... | collective-permute-start | bytes 589832 | tf_op jit(solution)/shard_map/ppermute | solution.py:324
  58.3 7.9 %collective-permute-start.7 = (f32[3,32,512]{2,1,0:T(8,128)S(1)}, f32[3,32,512]{2,1,0:T(8,128)S(1)}, u32[]{:S(2)}, u32[]{:S(2)}) collective-permute-start(f32[3,32,512]{2,1,0:T(8,128)S(1)} %get-tuple-element.17), channel_id=1, source_target_pairs={{4,0},{8,4},{12,8},{16,12},{20,16},{24,20},{28,24},{5,1},{9,5},{13... | collective-permute-start | bytes 589832 | tf_op jit(solution)/shard_map/ppermute | solution.py:324

commit v2 on v1

v2 whole, which is shorter than its diff:
```python
import functools
import math

import jax
import jax.numpy as jnp
import ml_dtypes
import numpy as np
from jax import lax
from jax.experimental import pallas as pl
from jax.experimental.pallas import tpu as pltpu
from jax.sharding import PartitionSpec as P

P_SIZE = 256
HALF = P_SIZE // 2
HALO = 32
LANES = 128
GROUPS = LANES // HALO
PAIR = 2

floor_amp = 0.5
ridge = 1.0

VMEM = pl.BlockSpec(memory_space=pltpu.VMEM)
SMEM = pl.BlockSpec(memory_space=pltpu.SMEM)
HBM = pl.BlockSpec(memory_space=pltpu.HBM)
PARAMS = pltpu.CompilerParams(vmem_limit_bytes=40 * 1024 * 1024)
ALONE = pltpu.CompilerParams(vmem_limit_bytes=60 * 1024 * 1024)
BUSY = pl.CostEstimate(flops=4_000_000_000, bytes_accessed=8_000_000, transcendentals=0)


def transform_tables():
    index = np.arange(HALF)
    plain = []
    for parity in (0, 1):
        angle = 2.0 * math.pi / P_SIZE * (index[:, None] * (2 * index[None, :] + parity) % P_SIZE)
        cos, sin = np.cos(angle), np.sin(angle)
        plain.append(np.block([[cos, -sin], [sin, cos]]) / math.sqrt(P_SIZE))
    parts = []
    for table in plain + [t.T for t in plain]:
        high = table.astype(np.float32).astype(ml_dtypes.bfloat16)
        low = (table - high.astype(np.float64)).astype(np.float32).astype(ml_dtypes.bfloat16)
        parts += [high, low]
    order = np.concatenate([np.arange(0, P_SIZE, 2), np.arange(1, P_SIZE, 2)])
    sort = np.zeros((P_SIZE, P_SIZE), np.float32)
    sort[np.arange(P_SIZE), order] = 1.0
    parts += [sort.astype(ml_dtypes.bfloat16), sort.T.astype(ml_dtypes.bfloat16)]
    return np.stack(parts)


def lane_index(rows):
    return lax.broadcasted_iota(jnp.int32, (rows, LANES), 1)


def pack_lanes(ref, rows, first):
    lane = lane_index(rows)
    packed = None
    for g in range(GROUPS):
        part = ref[g * rows : (g + 1) * rows, :]
        if g:
            part = pltpu.roll(part, HALO * g, 1)
        low = (first + HALO * g) % LANES
        mine = (lane >= low) & (lane < low + HALO)
        packed = part if packed is None else jnp.where(mine, part, packed)
    return packed


def unpack_lanes(packed, group):
    return pltpu.roll(packed, LANES - HALO * group, 1) if group else packed


def split(x):
    high = x.astype(jnp.bfloat16)
    return high, (x - high.astype(jnp.float32)).astype(jnp.bfloat16)


def product(left, right):
    return jnp.dot(left, right, preferred_element_type=jnp.float32)


def times_table(x, table, which):
    high, low = split(x)
    t_high, t_low = table[2 * which], table[2 * which + 1]
    return product(high, t_high) + (product(high, t_low) + product(low, t_high))


def table_times(table, which, x):
    high, low = split(x)
    t_high, t_low = table[2 * which], table[2 * which + 1]
    return product(t_high, high) + (product(t_low, high) + product(t_high, low))


def beside(*blocks):
    return jnp.concatenate(blocks, axis=1)


def below(*blocks):
    return jnp.concatenate(blocks, axis=0)


def ends(x):
    return x[:, :HALF], x[:, HALF:]


def forward_columns(exit_re, exit_im, table):
    re_lo, re_hi = ends(exit_re)
    im_lo, im_hi = ends(exit_im)
    even = times_table(beside(re_lo + re_hi, im_lo + im_hi), table, 0)
    odd = times_table(beside(re_lo - re_hi, im_lo - im_hi), table, 1)
    return even, odd


def forward_rows(even, odd, table):
    out = []
    for parity in (0, 1):
        if parity == 0:
            se, so = even[:HALF] + even[HALF:], odd[:HALF] + odd[HALF:]
        else:
            se, so = even[:HALF] - even[HALF:], odd[:HALF] - odd[HALF:]
        e_re, e_im = ends(se)
        o_re, o_im = ends(so)
        out.append(table_times(table, 2 + parity, below(beside(e_re, o_re), beside(e_im, o_im))))
    return out


def residual(far, frame):
    out = []
    for parity in (0, 1):
        re, im = far[parity][:HALF], far[parity][HALF:]
        level = jnp.maximum(re * re + im * im, floor_amp * floor_amp)
        inten = frame[parity * HALF : (parity + 1) * HALF]
        factor = 1.0 - inten * lax.rsqrt(inten * level)
        out.append(below(re * factor, im * factor))
    return out


def back_rows(res, table):
    first = table_times(table, 0, res[0])
    second = table_times(table, 1, res[1])
    upper, lower = first + second, first - second
    out = []
    for cols in (slice(0, HALF), slice(HALF, P_SIZE)):
        out.append(
            below(
                beside(upper[:HALF, cols], upper[HALF:, cols]),
                beside(lower[:HALF, cols], lower[HALF:, cols]),
            )
        )
    return out


def back_columns(parts, table):
    even = times_table(parts[0], table, 2)
    odd = times_table(parts[1], table, 3)
    lo, hi = even + odd, even - odd
    return beside(lo[:, :HALF], hi[:, :HALF]), beside(lo[:, HALF:], hi[:, HALF:])


def is_odd(axis):
    return lax.rem(lax.axis_index(axis), 2) == 1


def fetch(pairs, sems):
    copies = [pltpu.make_async_copy(far, near, sems.at[i]) for i, (far, near) in enumerate(pairs)]
    for copy in copies:
        copy.start()
    return copies


def finish_all(copies):
    for copy in copies:
        copy.wait()


def row_edges(obj_re, obj_im, to_inner, to_outer, sems):
    tile_r = obj_re.shape[0]
    odd = is_odd("row")
    low = pl.multiple_of(jnp.where(odd, 0, tile_r - HALO), 16)
    high = pl.multiple_of(jnp.where(odd, tile_r - HALO, 0), 16)
    pairs = []
    for k, ref in enumerate((obj_re, obj_im)):
        pairs.append((ref.at[pl.ds(high, HALO)], to_outer.at[k]))
        pairs.append((ref.at[pl.ds(low, HALO)], to_inner.at[k]))
    finish_all(fetch(pairs, sems))


def window_place(offsets, slot):
    row = pl.multiple_of(offsets[0, 0, slot, 0] + HALO, 16)
    col = offsets[0, 0, slot, 1] + LANES
    turn = lax.rem(col, LANES)
    return row, pl.multiple_of(col - turn, LANES), turn


def add_window(acc, layer, where, keep, term):
    row, base, _ = where
    lo, hi = ends(term)
    for t, part in enumerate((jnp.where(keep, lo, 0.0), hi, jnp.where(keep, 0.0, lo))):
        acc[layer, pl.ds(row, P_SIZE), pl.ds(base + t * LANES, LANES)] += part


def load_state(
    counts, offsets, obj_re, obj_im, probe_re_far, probe_im_far, frames_far, table_far,
    cells, acc, probe_re, probe_im, frames, table, power, sems,
):
    tile_r, tile_c = obj_re.shape
    inner = slice(HALO, HALO + tile_r)
    middle = slice(LANES, LANES + tile_c)
    copies = fetch(
        (
            (probe_re_far, probe_re),
            (probe_im_far, probe_im),
            (obj_re, cells.at[0, inner, middle]),
            (obj_im, cells.at[1, inner, middle]),
            (table_far, table),
            (frames_far, frames),
        ),
        sems,
    )
    acc[...] = jnp.zeros_like(acc)
    finish_all(copies[:2])
    power[...] = probe_re[...] * probe_re[...] + probe_im[...] * probe_im[...]
    lane = lane_index(P_SIZE)

    def step(slot, carry):
        where = window_place(offsets, slot)
        add_window(acc, 2, where, lane >= where[2], pltpu.roll(power[...], where[2], 1))
        return carry

    lax.fori_loop(0, counts[0, 0], step, 0)
    finish_all(copies[2:])


def fill_strip(strip, parts):
    done = 0
    for part in parts:
        strip[done : done + part.shape[0], :] = part
        done += part.shape[0]


def send_columns(to_left, to_right, to_inner, to_outer):
    odd = is_odd("col")
    to_inner[...] = jnp.where(odd, to_left, to_right)
    to_outer[...] = jnp.where(odd, to_right, to_left)


def received(by_inner, by_outer, axis):
    odd = is_odd(axis)
    before = jnp.where(odd, by_inner[0], by_outer[...])
    after = jnp.where(odd, by_outer[...], by_inner[1])
    return before, after


def pieces(packed, layers, rows):
    group_rows = layers * rows // GROUPS
    for g in range(GROUPS):
        part = unpack_lanes(packed, g)
        done = 0
        while done < group_rows:
            layer, row = divmod(g * group_rows + done, rows)
            size = min(group_rows - done, rows - row)
            yield layer, row, part[done : done + size]
            done += size


def row_halos(cells_in, acc, by_inner, by_outer, cells, to_inner, to_outer, strip):
    rows, width = acc.shape[1:]
    middle = slice(LANES, width - LANES)
    before, after = received(by_inner, by_outer, "row")
    for k in (0, 1):
        cells[k, 0:HALO, middle] = before[k]
        cells[k, rows - HALO : rows, middle] = after[k]
    group_rows = 3 * rows // GROUPS
    first, last = slice(LANES, 2 * LANES), slice(width - 2 * LANES, width - LANES)
    fill_strip(strip, (cells[0, :, first], cells[1, :, first], pltpu.roll(acc[2, :, 0:LANES], HALO, 1)))
    to_left = pack_lanes(strip, group_rows, 0)
    fill_strip(strip, (cells[0, :, last], cells[1, :, last], pltpu.roll(acc[2, :, width - LANES :], LANES - HALO, 1)))
    to_right = pack_lanes(strip, group_rows, LANES - HALO)
    send_columns(to_left, to_right, to_inner, to_outer)


def run_windows(wanted, counts, offsets, chosen, cells, acc, probe_re, probe_im, frames, table, order):
    tile_c = cells.shape[2] - 2 * LANES
    count = counts[0, 0]
    slots = range(offsets.shape[2])
    over = []
    for slot in slots:
        col = offsets[0, 0, slot, 1]
        over.append((col < 0) | (col > tile_c - P_SIZE))
    total = jnp.int32(0)
    for slot in slots:
        total += ((slot < count) & ~over[slot]).astype(jnp.int32)
    limit = jnp.where(total <= PAIR, total, jnp.where(total <= 2 * PAIR, PAIR, 2 * PAIR))
    seen, found = jnp.int32(0), jnp.int32(0)
    for slot in slots:
        live = slot < count
        mine = live & wanted(over[slot], seen, limit)

        @pl.when(mine)
        def _():
            order[found] = slot

        seen += (live & ~over[slot]).astype(jnp.int32)
        found += mine.astype(jnp.int32)

    lane = lane_index(P_SIZE)

    def load(slot):
        where = row, base, turn = window_place(offsets, slot)
        keep = lane >= turn
        w_re = pltpu.roll(probe_re[...], turn, 1)
        w_im = pltpu.roll(probe_im[...], turn, 1)
        patch = []
        for k in (0, 1):
            block = cells[k, pl.ds(row, P_SIZE), pl.ds(base, 3 * LANES)]
            patch.append(
                beside(jnp.where(keep, block[:, :LANES], block[:, 2 * LANES :]), block[:, LANES : 2 * LANES])
            )
        exit_re = w_re * patch[0] - w_im * patch[1]
        exit_im = w_re * patch[1] + w_im * patch[0]
        return (where, keep, w_re, w_im), exit_re, exit_im

    def frame_of(slot):
        sort, unsort = table[8], table[9]
        half = product(sort, frames[chosen[0, 0, slot]]).astype(jnp.bfloat16)
        return product(half, unsort)

    def place(at, back_re, back_im):
        where, keep, w_re, w_im = at
        add_window(acc, 0, where, keep, w_re * back_re + w_im * back_im)
        add_window(acc, 1, where, keep, w_re * back_im - w_im * back_re)

    def step(group):
        frame = [frame_of(slot) for slot in group]
        loaded = [load(slot) for slot in group]
        state = [forward_columns(x[1], x[2], table) for x in loaded]
        state = [forward_rows(*x, table) for x in state]
        state = [residual(x, f) for x, f in zip(state, frame)]
        state = [back_rows(x, table) for x in state]
        state = [back_columns(x, table) for x in state]
        for x, back in zip(loaded, state):
            place(x[0], *back)

    def pair_step(pair, carry):
        step([order[pair * PAIR + i] for i in range(PAIR)])
        return carry

    lax.fori_loop(0, found // PAIR, pair_step, 0)

    @pl.when(found % PAIR == 1)
    def _():
        step([order[found - 1]])


def windows_before(counts, offsets, chosen, cells, acc_in, probe_re, probe_im, frames, table, acc, order):
    run_windows(
        lambda over, seen, limit: ~over & (seen < limit),
        counts, offsets, chosen, cells, acc, probe_re, probe_im, frames, table, order,
    )


def windows_after(counts, offsets, chosen, cells, acc_in, probe_re, probe_im, frames, table, acc, order):
    run_windows(
        lambda over, seen, limit: ~over & (seen >= limit),
        counts, offsets, chosen, cells, acc, probe_re, probe_im, frames, table, order,
    )


def windows_over_edge(
    counts, offsets, chosen, cells_in, acc_in, probe_re, probe_im, frames, table, by_inner, by_outer,
    cells, acc, to_inner, to_outer, order, strip,
):
    rows, width = acc.shape[1:]
    before, after = received(by_inner, by_outer, "col")
    lane = lane_index(rows)[0:1]
    for layer, row, part in pieces(before, 3, rows):
        here = slice(row, row + part.shape[0])
        if layer < 2:
            cells[layer, here, 0:LANES] = part
        else:
            spilled = pltpu.roll(part, HALO, 1)
            acc[2, here, LANES : 2 * LANES] += jnp.where(lane < HALO, spilled, 0.0)
    for layer, row, part in pieces(after, 3, rows):
        here = slice(row, row + part.shape[0])
        if layer < 2:
            cells[layer, here, width - LANES :] = part
        else:
            spilled = pltpu.roll(part, LANES - HALO, 1)
            acc[2, here, width - 2 * LANES : width - LANES] += jnp.where(lane >= LANES - HALO, spilled, 0.0)
    run_windows(
        lambda over, seen, limit: over,
        counts, offsets, chosen, cells, acc, probe_re, probe_im, frames, table, order,
    )
    group_rows = 2 * rows // GROUPS
    fill_strip(strip, (acc[0, :, 0:LANES], acc[1, :, 0:LANES]))
    to_left = pack_lanes(strip, group_rows, LANES - HALO)
    fill_strip(strip, (acc[0, :, width - LANES :], acc[1, :, width - LANES :]))
    to_right = pack_lanes(strip, group_rows, 0)
    send_columns(to_left, to_right, to_inner, to_outer)


def row_spill(acc_in, by_inner, by_outer, acc, to_inner, to_outer):
    layers, rows, width = acc.shape
    before, after = received(by_inner, by_outer, "col")
    lane = lane_index(rows)[0:1]
    for layer, row, part in pieces(before, 2, rows):
        here = slice(row, row + part.shape[0])
        acc[layer, here, LANES : 2 * LANES] += jnp.where(lane < HALO, part, 0.0)
    for layer, row, part in pieces(after, 2, rows):
        here = slice(row, row + part.shape[0])
        acc[layer, here, width - 2 * LANES : width - LANES] += jnp.where(lane >= LANES - HALO, part, 0.0)
    odd = is_odd("row")
    for k in range(layers):
        up = acc[k, 0:HALO, LANES : width - LANES]
        down = acc[k, rows - HALO : rows, LANES : width - LANES]
        to_inner[k] = jnp.where(odd, up, down)
        to_outer[k] = jnp.where(odd, down, up)


def finish(cells, acc, by_inner, by_outer, new_re, new_im):
    layers, rows, width = acc.shape
    tile_r = rows - 2 * HALO
    middle = slice(LANES, width - LANES)
    before, after = received(by_inner, by_outer, "row")
    for start, size, extra in (
        (0, HALO, before),
        (HALO, tile_r - 2 * HALO, None),
        (tile_r - HALO, HALO, after),
    ):
        here = slice(HALO + start, HALO + start + size)
        part = [acc[k, here, middle] for k in range(layers)]
        if extra is not None:
            part = [part[k] + extra[k] for k in range(layers)]
        scale = 1.0 / (part[2] + ridge)
        new_re[start : start + size, :] = cells[0, here, middle] - part[0] * scale
        new_im[start : start + size, :] = cells[1, here, middle] - part[1] * scale


def swap(to_inner, to_outer, axis):
    devices = lax.axis_size(axis)
    groups = [[i, i + 1] for i in range(0, devices, 2)]
    pairs = [(i, i + 1) for i in range(1, devices - 1, 2)]
    by_inner = lax.all_gather(to_inner, axis, axis_index_groups=groups)
    by_outer = lax.ppermute(to_outer, axis, pairs + [(j, i) for i, j in pairs])
    return by_inner, by_outer


def f32(*shape):
    return jax.ShapeDtypeStruct(shape, jnp.float32)


def shards(object_re, object_im, probe_re, probe_im, frames, counts, offsets, frame_index):
    tile_r, tile_c = object_re.shape
    rows, width = tile_r + 2 * HALO, tile_c + 2 * LANES
    layers = 3
    slots = offsets.shape[2]
    table = jnp.asarray(transform_tables())
    frames = frames.reshape(frames.shape[2:])
    cells_shape, acc_shape = f32(2, rows, width), f32(layers, rows, width)
    dma = pltpu.SemaphoreType.DMA

    edge = f32(2, HALO, tile_c)
    to_inner, to_outer = pl.pallas_call(
        row_edges,
        out_shape=(edge, edge),
        in_specs=[HBM] * 2,
        out_specs=(VMEM, VMEM),
        scratch_shapes=[dma((4,))],
        compiler_params=ALONE,
        name="row_edges",
    )(object_re, object_im)
    by_inner, by_outer = swap(to_inner, to_outer, "row")

    cells, acc, *fixed = pl.pallas_call(
        load_state,
        out_shape=(
            cells_shape, acc_shape, f32(*probe_re.shape), f32(*probe_im.shape),
            jax.ShapeDtypeStruct(frames.shape, frames.dtype), jax.ShapeDtypeStruct(table.shape, table.dtype),
        ),
        in_specs=[SMEM] * 2 + [HBM] * 6,
        out_specs=(VMEM,) * 6,
        scratch_shapes=[pltpu.VMEM(probe_re.shape, jnp.float32), dma((6,))],
        compiler_params=PARAMS,
        cost_estimate=BUSY,
        name="load_state",
    )(counts, offsets, object_re, object_im, probe_re, probe_im, frames, table)

    strip = pltpu.VMEM((3 * rows, LANES), jnp.float32)
    packed = f32(3 * rows // GROUPS, LANES)
    cells, to_inner, to_outer = pl.pallas_call(
        row_halos,
        out_shape=(cells_shape, packed, packed),
        in_specs=[VMEM] * 4,
        out_specs=(VMEM,) * 3,
        scratch_shapes=[strip],
        input_output_aliases={0: 0},
        compiler_params=PARAMS,
        name="row_halos",
    )(cells, acc, by_inner, by_outer)
    by_inner, by_outer = swap(to_inner, to_outer, "col")

    order = pltpu.SMEM((slots,), jnp.int32)
    scalars = (counts, offsets, frame_index)
    acc = pl.pallas_call(
        windows_before,
        out_shape=acc_shape,
        in_specs=[SMEM] * 3 + [VMEM] * 6,
        out_specs=VMEM,
        scratch_shapes=[order],
        input_output_aliases={4: 0},
        compiler_params=PARAMS,
        cost_estimate=BUSY,
        name="windows_before",
    )(*scalars, cells, acc, *fixed)

    packed = f32(2 * rows // GROUPS, LANES)
    cells, acc, to_inner, to_outer = pl.pallas_call(
        windows_over_edge,
        out_shape=(cells_shape, acc_shape, packed, packed),
        in_specs=[SMEM] * 3 + [VMEM] * 8,
        out_specs=(VMEM,) * 4,
        scratch_shapes=[order, strip],
        input_output_aliases={3: 0, 4: 1},
        compiler_params=PARAMS,
        cost_estimate=BUSY,
        name="windows_over_edge",
    )(*scalars, cells, acc, *fixed, by_inner, by_outer)
    by_inner, by_outer = swap(to_inner, to_outer, "col")

    acc = pl.pallas_call(
        windows_after,
        out_shape=acc_shape,
        in_specs=[SMEM] * 3 + [VMEM] * 6,
        out_specs=VMEM,
        scratch_shapes=[order],
        input_output_aliases={4: 0},
        compiler_params=PARAMS,
        cost_estimate=BUSY,
        name="windows_after",
    )(*scalars, cells, acc, *fixed)

    edge = f32(layers, HALO, tile_c)
    acc, to_inner, to_outer = pl.pallas_call(
        row_spill,
        out_shape=(acc_shape, edge, edge),
        in_specs=[VMEM] * 3,
        out_specs=(VMEM,) * 3,
        input_output_aliases={0: 0},
        compiler_params=PARAMS,
        name="row_spill",
    )(acc, by_inner, by_outer)
    by_inner, by_outer = swap(to_inner, to_outer, "row")

    return pl.pallas_call(
        finish,
        out_shape=(f32(tile_r, tile_c), f32(tile_r, tile_c)),
        in_specs=[VMEM] * 4,
        out_specs=(VMEM, VMEM),
        compiler_params=PARAMS,
        name="finish",
    )(cells, acc, by_inner, by_outer)


def solution(mesh):
    return jax.shard_map(
        shards,
        mesh=mesh,
        in_specs=(
            P("row", "col"),
            P("row", "col"),
            P(),
            P(),
            P("row", "col", None, None, None),
            P("row", "col"),
            P("row", "col", None, None),
            P("row", "col", None),
        ),
        out_specs=(P("row", "col"), P("row", "col")),
        check_vma=False,
    )
```

time: 68 us -> 55.4 us (0.81)
  the two profiles are of different devices: /device:TPU:3 before, /device:TPU:1 now
where the time goes in v2:
time: 55.4 us; the launch traced here: 55.5 us
  blocking collectives  17.8 us (32%)
  Pallas kernels  16.3 us (29%)
  starting transfers between devices  8.66 us (16%)
  local copies, waits for them, and re-layouts  7.47 us (13%)
  waiting for transfers between devices  3.89 us (7%)
  between operations  1.4 us (3%)
    all_gather x4, blocking collectives, swap(): by_inner = lax.all_gather(to_inner, axis, axis_index_groups=groups)  17.8 us
    ppermute x4, starting transfers between devices, swap(): by_outer = lax.ppermute(to_outer, axis, pairs + [(j, i) for i, j in pairs])  8.66 us
    unnamed x17, local copies, waits for them, and re-layouts  7.47 us
    pallas_call x1, Pallas kernels, shards(): pl.pallas_call(windows_over_edge, out_shape=(cells_shape, acc_shape, pack...  3.9 us
    ppermute x4, waiting for transfers between devices, swap(): by_outer = lax.ppermute(to_outer, axis, pairs + [(j, i) for i, j in pairs])  3.89 us
    pallas_call x1, Pallas kernels, shards(): pl.pallas_call(windows_after, out_shape=acc_shape, in_specs=[SMEM] * 3 +...  3.11 us
    pallas_call x1, Pallas kernels, shards(): pl.pallas_call(windows_before, out_shape=acc_shape, in_specs=[SMEM] * 3 +...  3.11 us
    pallas_call x1, Pallas kernels, shards(): pl.pallas_call(load_state, out_shape=(cells_shape, acc_shape, f32(*probe_...  2.27 us
  transfers between devices with their start and end apart: 4, of which 1 were waited for; matrix products, arithmetic and copies ran while one was open for 1% of the time, Pallas kernels for 15%

profile of v2, /device:TPU:1, one launch (start us, length us, event | category | flops | bytes accessed | tf_op | source)
XLA Modules:
  0.0 55.5 jit_solution(18331106787832613624)
XLA Ops:
  0.6 1.7 %row_edges.1 = (f32[2,32,512]{2,1,0:T(8,128)}, f32[2,32,512]{2,1,0:T(8,128)}) custom-call(f32[384,512]{1,0:T(8,128)} %obj_re.3, f32[384,512]{1,0:T(8,128)} %obj_im.3), custom_call_target="tpu_custom_call" | custom-call | tf_op jit(solution)/shard_map/row_edges/pallas_call | solution.py:461
  2.3 4.5 %collective-permute-start = (f32[2,32,512]{2,1,0:T(8,128)}, f32[2,32,512]{2,1,0:T(8,128)S(1)}, u32[]{:S(2)}, u32[]{:S(2)}) collective-permute-start(f32[2,32,512]{2,1,0:T(8,128)} %get-tuple-element.23), channel_id=1, source_target_pairs={{4,8},{12,16},{20,24},{8,4},{16,12},{24,20},{5,9},{13,17},{21,25},... | collective-permute-start | bytes 393224 | tf_op jit(solution)/shard_map/ppermute | solution.py:442
  7.5 0.8 %copy.23.offsets = s32[1,1,8,2]{3,2,1,0:T(8,128)S(1)} copy(s32[1,1,8,2]{2,3,1,0:T(2,128)} %param.15) | data formatting | bytes 128 | tf_op args[6]
  8.2 0.0 copy-start
  8.2 1.1 %copy-done = f32[384,512]{1,0:T(8,128)S(1)} copy-done((f32[384,512]{1,0:T(8,128)S(1)}, f32[384,512]{1,0:T(8,128)}, u32[]{:S(2)}) %copy-start) | copy-done | bytes 786456
  9.4 0.0 copy-start.1
  9.4 1.1 %copy-done.1 = f32[384,512]{1,0:T(8,128)S(1)} copy-done((f32[384,512]{1,0:T(8,128)S(1)}, f32[384,512]{1,0:T(8,128)}, u32[]{:S(2)}) %copy-start.1) | copy-done | bytes 786456
  10.5 0.0 copy-start.2
  10.5 1.2 %copy-done.2 = bf16[1,1,8,256,256]{4,3,2,1,0:T(8,128)(2,1)S(1)} copy-done((bf16[1,1,8,256,256]{4,3,2,1,0:T(8,128)(2,1)S(1)}, bf16[1,1,8,256,256]{4,3,2,1,0:T(8,128)(2,1)}, u32[]{:S(2)}) %copy-start.2) | copy-done | bytes 1048600
  11.7 0.0 copy-start.3
  11.7 0.9 %copy-done.3 = f32[256,256]{1,0:T(8,128)S(1)} copy-done((f32[256,256]{1,0:T(8,128)S(1)}, f32[256,256]{1,0:T(8,128)}, u32[]{:S(2)}) %copy-start.3) | copy-done | bytes 262168
  12.7 0.0 copy-start.4
  12.7 0.9 %copy-done.4 = f32[256,256]{1,0:T(8,128)S(1)} copy-done((f32[256,256]{1,0:T(8,128)S(1)}, f32[256,256]{1,0:T(8,128)}, u32[]{:S(2)}) %copy-start.4) | copy-done | bytes 262168
  13.6 0.0 copy-start.6
  13.6 1.3 %copy-done.6 = bf16[10,256,256]{2,1,0:T(8,128)(2,1)S(1)} copy-done((bf16[10,256,256]{2,1,0:T(8,128)(2,1)S(1)}, bf16[10,256,256]{2,1,0:T(8,128)(2,1)}, u32[]{:S(2)}) %copy-start.6) | copy-done | bytes 1310744
  14.9 0.0 copy-start.7
  15.0 2.3 %load_state.1 = (f32[2,448,768]{2,1,0:T(8,128)S(1)}, f32[3,448,768]{2,1,0:T(8,128)S(1)}, f32[256,256]{1,0:T(8,128)S(1)}, f32[256,256]{1,0:T(8,128)S(1)}, bf16[8,...) custom-call(s32[1,1]{1,0:T(1,128)S(6)} %copy.31.counts, s32[1,1,8,2]{3,2,1,0:T(8,128)S(1)} %copy.23.offsets, ...), custom_call_target="tpu_custom_call" | custom-call | flops 4000000000 | bytes 8000000 | tf_op jit(solution)/shard_map/load_state/pallas_call | solution.py:472
  17.2 0.0 copy-start.5
  17.2 0.0 copy-done.7
  17.2 2.0 %all-gather = f32[4,32,512]{2,1,0:T(8,128)S(1)} all-gather(f32[2,32,512]{2,1,0:T(8,128)S(1)} %copy-done.7), channel_id=2, replica_groups={{0,4},{8,12},{16,20},{24,28},{1,5},{9,13},{17,21},{25,29},{2,6},{10,14}..., dimensions={0}, use_global_device_ids=true | all-gather | bytes 393216 | tf_op jit(solution)/shard_map/all_gather | solution.py:441
  19.2 0.0 collective-permute-done.by_outer
  19.2 0.5 row_halos.1
  19.7 0.7 %collective-permute-start.1 = (f32[336,128]{1,0:T(8,128)S(1)}, f32[336,128]{1,0:T(8,128)S(1)}, u32[]{:S(2)}, u32[]{:S(2)}) collective-permute-start(f32[336,128]{1,0:T(8,128)S(1)} %get-tuple-element.30), channel_id=1, source_target_pairs={{1,2},{2,1},{5,6},{6,5},{9,10},{10,9},{13,14},{14,13},{17,18},{18,... | collective-permute-start | bytes 516104 | tf_op jit(solution)/shard_map/ppermute | solution.py:442
  20.4 0.0 copy-done.5
  20.4 3.1 %windows_before.1.acc_in = f32[3,448,768]{2,1,0:T(8,128)S(1)} custom-call(s32[1,1]{1,0:T(1,128)S(6)} %copy.31.counts, s32[1,1,8,2]{3,2,1,0:T(8,128)S(1)} %copy.23.offsets, s32[1,1,8]{2,1,0:T(1,128)S(1)} %copy-done.5, f32[2,448,768]{2,1,0:T(8,128)S(1)} %get-tuple-element.24.cells.cells_in, ...), custom_call_target="tpu_custom_call", output_to_operand_aliasing={{}: (4, {})} | custom-call | flops 4000000000 | bytes 8000000 | tf_op jit(solution)/shard_map/windows_before/pallas_call | solution.py:502
  23.5 8.2 %all-gather.1 = f32[672,128]{1,0:T(8,128)S(1)} all-gather(f32[336,128]{1,0:T(8,128)S(1)} %get-tuple-element.29), channel_id=3, replica_groups={{0,1},{2,3},{4,5},{6,7},{8,9},{10,11},{12,13},{14,15},{16,17},{18,19},{..., dimensions={0}, use_global_device_ids=true | all-gather | bytes 516096 | tf_op jit(solution)/shard_map/all_gather | solution.py:441
  31.7 0.0 collective-permute-done.1.by_outer
  31.7 3.9 %windows_over_edge.1 = (f32[2,448,768]{2,1,0:T(8,128)S(1)}, f32[3,448,768]{2,1,0:T(8,128)S(1)}, f32[224,128]{1,0:T(8,128)S(1)}, f32[224,128]{1,0:T(8,128)S(1)}) custom-call(s32[1,1]{1,0:T(1,128)S(6)} %copy.31.counts, s32[1,1,8,2]{3,2,1,0:T(8,128)S(1)} %copy.23.offsets, s32[1,1,8]{2,1,0:T(1,128)S(1)} %copy-done.5, ...), custom_call_target="tpu_custom_call", output_to_operand_aliasing={{0}: (3, {}), {1}: (4, {})} | custom-call | flops 4000000000 | bytes 8000000 | tf_op jit(solution)/shard_map/windows_over_edge/pallas_call | solution.py:515
  35.6 0.7 %collective-permute-start.2 = (f32[224,128]{1,0:T(8,128)S(1)}, f32[224,128]{1,0:T(8,128)S(1)}, u32[]{:S(2)}, u32[]{:S(2)}) collective-permute-start(f32[224,128]{1,0:T(8,128)S(1)} %get-tuple-element.34), channel_id=1, source_target_pairs={{1,2},{2,1},{5,6},{6,5},{9,10},{10,9},{13,14},{14,13},{17,18},{18,... | collective-permute-start | bytes 344072 | tf_op jit(solution)/shard_map/ppermute | solution.py:442
  36.3 3.1 %windows_after.1.acc_in = f32[3,448,768]{2,1,0:T(8,128)S(1)} custom-call(s32[1,1]{1,0:T(1,128)S(6)} %copy.31.counts, s32[1,1,8,2]{3,2,1,0:T(8,128)S(1)} %copy.23.offsets, s32[1,1,8]{2,1,0:T(1,128)S(1)} %copy-done.5, f32[2,448,768]{2,1,0:T(8,128)S(1)} %get-tuple-element.31.cells, ...), custom_call_target="tpu_custom_call", output_to_operand_aliasing={{}: (4, {})} | custom-call | flops 4000000000 | bytes 8000000 | tf_op jit(solution)/shard_map/windows_after/pallas_call | solution.py:528
  39.4 5.5 %all-gather.2 = f32[448,128]{1,0:T(8,128)S(1)} all-gather(f32[224,128]{1,0:T(8,128)S(1)} %get-tuple-element.33), channel_id=4, replica_groups={{0,1},{2,3},{4,5},{6,7},{8,9},{10,11},{12,13},{14,15},{16,17},{18,19},{..., dimensions={0}, use_global_device_ids=true | all-gather | bytes 344064 | tf_op jit(solution)/shard_map/all_gather | solution.py:441
  44.9 0.0 collective-permute-done.2.by_outer
  44.9 0.3 row_spill.1
  45.2 2.8 %collective-permute-start.3 = (f32[3,32,512]{2,1,0:T(8,128)S(1)}, f32[3,32,512]{2,1,0:T(8,128)S(1)}, u32[]{:S(2)}, u32[]{:S(2)}) collective-permute-start(f32[3,32,512]{2,1,0:T(8,128)S(1)} %get-tuple-element.37), channel_id=1, source_target_pairs={{4,8},{12,16},{20,24},{8,4},{16,12},{24,20},{5,9},{13,17},{21,25},... | collective-permute-start | bytes 589832 | tf_op jit(solution)/shard_map/ppermute | solution.py:442
  48.0 2.1 %all-gather.3 = f32[6,32,512]{2,1,0:T(8,128)S(1)} all-gather(f32[3,32,512]{2,1,0:T(8,128)S(1)} %get-tuple-element.36), channel_id=5, replica_groups={{0,4},{8,12},{16,20},{24,28},{1,5},{9,13},{17,21},{25,29},{2,6},{10,14}..., dimensions={0}, use_global_device_ids=true | all-gather | bytes 589824 | tf_op jit(solution)/shard_map/all_gather | solution.py:441
  50.1 3.9 %collective-permute-done.3.by_outer = f32[3,32,512]{2,1,0:T(8,128)S(1)} collective-permute-done((f32[3,32,512]{2,1,0:T(8,128)S(1)}, f32[3,32,512]{2,1,0:T(8,128)S(1)}, u32[]{:S(2)}, u32[]{:S(2)}) %collective-permute-start.3) | collective-permute-done | bytes 196640 | tf_op jit(solution)/shard_map/ppermute | solution.py:442
  54.0 1.5 %finish.1 = (f32[384,512]{1,0:T(8,128)}, f32[384,512]{1,0:T(8,128)}) custom-call(f32[2,448,768]{2,1,0:T(8,128)S(1)} %get-tuple-element.31.cells, f32[3,448,768]{2,1,0:T(8,128)S(1)} %get-tuple-element.35.acc, f32[2,3,32,512]{3,2,1,0:T(8,128)S(1)} %bitcast.5, f32[3,32,512]{2,1,0:T(8,128)S(1)} %collective-permute-done.3.by_outer), custom_call_target="tpu_custom_call" | custom-call | tf_op jit(solution)/shard_map/finish/pallas_call | solution.py:552
Async XLA Ops:
  2.3 16.9 %collective-permute-start = (f32[2,32,512]{2,1,0:T(8,128)}, f32[2,32,512]{2,1,0:T(8,128)S(1)}, u32[]{:S(2)}, u32[]{:S(2)}) collective-permute-start(f32[2,32,512]{2,1,0:T(8,128)} %get-tuple-element.23), channel_id=1, source_target_pairs={{4,8},{12,16},{20,24},{8,4},{16,12},{24,20},{5,9},{13,17},{21,25},... | collective-permute-start | bytes 393224 | tf_op jit(solution)/shard_map/ppermute | solution.py:442
  8.2 1.1 %copy-start = (f32[384,512]{1,0:T(8,128)S(1)}, f32[384,512]{1,0:T(8,128)}, u32[]{:S(2)}) copy-start(f32[384,512]{1,0:T(8,128)} %obj_re.3) | copy-start | bytes 2359300
  9.4 1.1 %copy-start.1 = (f32[384,512]{1,0:T(8,128)S(1)}, f32[384,512]{1,0:T(8,128)}, u32[]{:S(2)}) copy-start(f32[384,512]{1,0:T(8,128)} %obj_im.3) | copy-start | bytes 2359300
  10.5 1.2 %copy-start.2 = (bf16[1,1,8,256,256]{4,3,2,1,0:T(8,128)(2,1)S(1)}, bf16[1,1,8,256,256]{4,3,2,1,0:T(8,128)(2,1)}, u32[]{:S(2)}) copy-start(bf16[1,1,8,256,256]{4,3,2,1,0:T(8,128)(2,1)} %param.13) | copy-start | bytes 3145732
  11.7 0.9 %copy-start.3 = (f32[256,256]{1,0:T(8,128)S(1)}, f32[256,256]{1,0:T(8,128)}, u32[]{:S(2)}) copy-start(f32[256,256]{1,0:T(8,128)} %probe_re_far.1) | copy-start | bytes 786436
  12.7 0.9 %copy-start.4 = (f32[256,256]{1,0:T(8,128)S(1)}, f32[256,256]{1,0:T(8,128)}, u32[]{:S(2)}) copy-start(f32[256,256]{1,0:T(8,128)} %probe_im_far.1) | copy-start | bytes 786436
  13.6 1.3 %copy-start.6 = (bf16[10,256,256]{2,1,0:T(8,128)(2,1)S(1)}, bf16[10,256,256]{2,1,0:T(8,128)(2,1)}, u32[]{:S(2)}) copy-start(bf16[10,256,256]{2,1,0:T(8,128)(2,1)} %constant.2.clone.table_far) | copy-start | bytes 3932164
  14.9 2.3 %copy-start.7 = (f32[2,32,512]{2,1,0:T(8,128)S(1)}, f32[2,32,512]{2,1,0:T(8,128)}, u32[]{:S(2)}) copy-start(f32[2,32,512]{2,1,0:T(8,128)} %get-tuple-element.22) | copy-start | bytes 393220
  17.2 3.2 %copy-start.5 = (s32[1,1,8]{2,1,0:T(1,128)S(1)}, s32[1,1,8]{2,1,0:T(1,128)}, u32[]{:S(2)}) copy-start(s32[1,1,8]{2,1,0:T(1,128)} %chosen.5) | copy-start | bytes 100
  19.7 12.0 %collective-permute-start.1 = (f32[336,128]{1,0:T(8,128)S(1)}, f32[336,128]{1,0:T(8,128)S(1)}, u32[]{:S(2)}, u32[]{:S(2)}) collective-permute-start(f32[336,128]{1,0:T(8,128)S(1)} %get-tuple-element.30), channel_id=1, source_target_pairs={{1,2},{2,1},{5,6},{6,5},{9,10},{10,9},{13,14},{14,13},{17,18},{18,... | collective-permute-start | bytes 516104 | tf_op jit(solution)/shard_map/ppermute | solution.py:442
  35.6 9.3 %collective-permute-start.2 = (f32[224,128]{1,0:T(8,128)S(1)}, f32[224,128]{1,0:T(8,128)S(1)}, u32[]{:S(2)}, u32[]{:S(2)}) collective-permute-start(f32[224,128]{1,0:T(8,128)S(1)} %get-tuple-element.34), channel_id=1, source_target_pairs={{1,2},{2,1},{5,6},{6,5},{9,10},{10,9},{13,14},{14,13},{17,18},{18,... | collective-permute-start | bytes 344072 | tf_op jit(solution)/shard_map/ppermute | solution.py:442
  45.2 8.8 %collective-permute-start.3 = (f32[3,32,512]{2,1,0:T(8,128)S(1)}, f32[3,32,512]{2,1,0:T(8,128)S(1)}, u32[]{:S(2)}, u32[]{:S(2)}) collective-permute-start(f32[3,32,512]{2,1,0:T(8,128)S(1)} %get-tuple-element.37), channel_id=1, source_target_pairs={{4,8},{12,16},{20,24},{8,4},{16,12},{24,20},{5,9},{13,17},{21,25},... | collective-permute-start | bytes 589832 | tf_op jit(solution)/shard_map/ppermute | solution.py:442

commit v3 on v2

--- a/solution.py
+++ b/solution.py
@@ -24,7 +24,6 @@
 SMEM = pl.BlockSpec(memory_space=pltpu.SMEM)
 HBM = pl.BlockSpec(memory_space=pltpu.HBM)
 PARAMS = pltpu.CompilerParams(vmem_limit_bytes=40 * 1024 * 1024)
-ALONE = pltpu.CompilerParams(vmem_limit_bytes=60 * 1024 * 1024)
 BUSY = pl.CostEstimate(flops=4_000_000_000, bytes_accessed=8_000_000, transcendentals=0)
 
 
@@ -198,8 +197,8 @@
 
 
 def load_state(
-    counts, offsets, obj_re, obj_im, probe_re_far, probe_im_far, frames_far, table_far,
-    cells, acc, probe_re, probe_im, frames, table, power, sems,
+    obj_re, obj_im, probe_re_far, probe_im_far, frames_far, table_far,
+    cells, probe_re, probe_im, frames, table, sems,
 ):
     tile_r, tile_c = obj_re.shape
     inner = slice(HALO, HALO + tile_r)
@@ -215,18 +214,7 @@
         ),
         sems,
     )
-    acc[...] = jnp.zeros_like(acc)
-    finish_all(copies[:2])
-    power[...] = probe_re[...] * probe_re[...] + probe_im[...] * probe_im[...]
-    lane = lane_index(P_SIZE)
-
-    def step(slot, carry):
-        where = window_place(offsets, slot)
-        add_window(acc, 2, where, lane >= where[2], pltpu.roll(power[...], where[2], 1))
-        return carry
-
-    lax.fori_loop(0, counts[0, 0], step, 0)
-    finish_all(copies[2:])
+    finish_all(copies)
 
 
 def fill_strip(strip, parts):
@@ -244,9 +232,11 @@
 
 def received(by_inner, by_outer, axis):
     odd = is_odd(axis)
-    before = jnp.where(odd, by_inner[0], by_outer[...])
-    after = jnp.where(odd, by_outer[...], by_inner[1])
-    return before, after
+    if len(by_inner.shape) > len(by_outer.shape):
+        before, after = by_inner[0], by_inner[1]
+    else:
+        before = after = by_inner[...]
+    return jnp.where(odd, before, by_outer[...]), jnp.where(odd, by_outer[...], after)
 
 
 def pieces(packed, layers, rows):
@@ -261,18 +251,18 @@
             done += size
 
 
-def row_halos(cells_in, acc, by_inner, by_outer, cells, to_inner, to_outer, strip):
-    rows, width = acc.shape[1:]
+def row_halos(cells_in, by_inner, by_outer, cells, to_inner, to_outer, strip):
+    rows, width = cells.shape[1:]
     middle = slice(LANES, width - LANES)
     before, after = received(by_inner, by_outer, "row")
     for k in (0, 1):
         cells[k, 0:HALO, middle] = before[k]
         cells[k, rows - HALO : rows, middle] = after[k]
-    group_rows = 3 * rows // GROUPS
+    group_rows = 2 * rows // GROUPS
     first, last = slice(LANES, 2 * LANES), slice(width - 2 * LANES, width - LANES)
-    fill_strip(strip, (cells[0, :, first], cells[1, :, first], pltpu.roll(acc[2, :, 0:LANES], HALO, 1)))
+    fill_strip(strip, (cells[0, :, first], cells[1, :, first]))
     to_left = pack_lanes(strip, group_rows, 0)
-    fill_strip(strip, (cells[0, :, last], cells[1, :, last], pltpu.roll(acc[2, :, width - LANES :], LANES - HALO, 1)))
+    fill_strip(strip, (cells[0, :, last], cells[1, :, last]))
     to_right = pack_lanes(strip, group_rows, LANES - HALO)
     send_columns(to_left, to_right, to_inner, to_outer)
 
@@ -350,7 +340,17 @@
         step([order[found - 1]])
 
 
-def windows_before(counts, offsets, chosen, cells, acc_in, probe_re, probe_im, frames, table, acc, order):
+def windows_before(counts, offsets, chosen, cells, probe_re, probe_im, frames, table, acc, order, power):
+    acc[...] = jnp.zeros_like(acc)
+    power[...] = probe_re[...] * probe_re[...] + probe_im[...] * probe_im[...]
+    lane = lane_index(P_SIZE)
+
+    def step(slot, carry):
+        where = window_place(offsets, slot)
+        add_window(acc, 2, where, lane >= where[2], pltpu.roll(power[...], where[2], 1))
+        return carry
+
+    lax.fori_loop(0, counts[0, 0], step, 0)
     run_windows(
         lambda over, seen, limit: ~over & (seen < limit),
         counts, offsets, chosen, cells, acc, probe_re, probe_im, frames, table, order,
@@ -370,29 +370,19 @@
 ):
     rows, width = acc.shape[1:]
     before, after = received(by_inner, by_outer, "col")
-    lane = lane_index(rows)[0:1]
-    for layer, row, part in pieces(before, 3, rows):
-        here = slice(row, row + part.shape[0])
-        if layer < 2:
-            cells[layer, here, 0:LANES] = part
-        else:
-            spilled = pltpu.roll(part, HALO, 1)
-            acc[2, here, LANES : 2 * LANES] += jnp.where(lane < HALO, spilled, 0.0)
-    for layer, row, part in pieces(after, 3, rows):
-        here = slice(row, row + part.shape[0])
-        if layer < 2:
-            cells[layer, here, width - LANES :] = part
-        else:
-            spilled = pltpu.roll(part, LANES - HALO, 1)
-            acc[2, here, width - 2 * LANES : width - LANES] += jnp.where(lane >= LANES - HALO, spilled, 0.0)
+    for layer, row, part in pieces(before, 2, rows):
+        cells[layer, row : row + part.shape[0], 0:LANES] = part
+    for layer, row, part in pieces(after, 2, rows):
+        cells[layer, row : row + part.shape[0], width - LANES :] = part
     run_windows(
         lambda over, seen, limit: over,
         counts, offsets, chosen, cells, acc, probe_re, probe_im, frames, table, order,
     )
-    group_rows = 2 * rows // GROUPS
-    fill_strip(strip, (acc[0, :, 0:LANES], acc[1, :, 0:LANES]))
+    layers = acc.shape[0]
+    group_rows = layers * rows // GROUPS
+    fill_strip(strip, [acc[k, :, 0:LANES] for k in range(layers)])
     to_left = pack_lanes(strip, group_rows, LANES - HALO)
-    fill_strip(strip, (acc[0, :, width - LANES :], acc[1, :, width - LANES :]))
+    fill_strip(strip, [acc[k, :, width - LANES :] for k in range(layers)])
     to_right = pack_lanes(strip, group_rows, 0)
     send_columns(to_left, to_right, to_inner, to_outer)
 
@@ -401,10 +391,10 @@
     layers, rows, width = acc.shape
     before, after = received(by_inner, by_outer, "col")
     lane = lane_index(rows)[0:1]
-    for layer, row, part in pieces(before, 2, rows):
+    for layer, row, part in pieces(before, layers, rows):
         here = slice(row, row + part.shape[0])
         acc[layer, here, LANES : 2 * LANES] += jnp.where(lane < HALO, part, 0.0)
-    for layer, row, part in pieces(after, 2, rows):
+    for layer, row, part in pieces(after, layers, rows):
         here = slice(row, row + part.shape[0])
         acc[layer, here, width - 2 * LANES : width - LANES] += jnp.where(lane >= LANES - HALO, part, 0.0)
     odd = is_odd("row")
@@ -434,13 +424,20 @@
         new_im[start : start + size, :] = cells[1, here, middle] - part[1] * scale
 
 
-def swap(to_inner, to_outer, axis):
+def swap(to_inner, to_outer, axis, gather):
     devices = lax.axis_size(axis)
-    groups = [[i, i + 1] for i in range(0, devices, 2)]
-    pairs = [(i, i + 1) for i in range(1, devices - 1, 2)]
-    by_inner = lax.all_gather(to_inner, axis, axis_index_groups=groups)
-    by_outer = lax.ppermute(to_outer, axis, pairs + [(j, i) for i, j in pairs])
+    inner = [(i, i + 1) for i in range(0, devices, 2)]
+    outer = [(i, i + 1) for i in range(1, devices - 1, 2)]
+    by_outer = lax.ppermute(to_outer, axis, outer + [(j, i) for i, j in outer])
+    if gather:
+        by_inner = lax.all_gather(to_inner, axis, axis_index_groups=[list(pair) for pair in inner])
+    else:
+        by_inner = lax.ppermute(to_inner, axis, inner + [(j, i) for i, j in inner])
     return by_inner, by_outer
+
+
+def far(x):
+    return pltpu.with_memory_space_constraint(x, pltpu.HBM)
 
 
 def f32(*shape):
@@ -462,56 +459,55 @@
         row_edges,
         out_shape=(edge, edge),
         in_specs=[HBM] * 2,
-        out_specs=(VMEM, VMEM),
+        out_specs=(HBM, VMEM),
         scratch_shapes=[dma((4,))],
-        compiler_params=ALONE,
+        compiler_params=PARAMS,
         name="row_edges",
-    )(object_re, object_im)
-    by_inner, by_outer = swap(to_inner, to_outer, "row")
-
-    cells, acc, *fixed = pl.pallas_call(
+    )(far(object_re), far(object_im))
+    by_inner, by_outer = swap(to_inner, to_outer, "row", True)
+
+    cells, *fixed = pl.pallas_call(
         load_state,
         out_shape=(
-            cells_shape, acc_shape, f32(*probe_re.shape), f32(*probe_im.shape),
+            cells_shape, f32(*probe_re.shape), f32(*probe_im.shape),
             jax.ShapeDtypeStruct(frames.shape, frames.dtype), jax.ShapeDtypeStruct(table.shape, table.dtype),
         ),
-        in_specs=[SMEM] * 2 + [HBM] * 6,
-        out_specs=(VMEM,) * 6,
-        scratch_shapes=[pltpu.VMEM(probe_re.shape, jnp.float32), dma((6,))],
+        in_specs=[HBM] * 6,
+        out_specs=(VMEM,) * 5,
+        scratch_shapes=[dma((6,))],
         compiler_params=PARAMS,
         cost_estimate=BUSY,
         name="load_state",
-    )(counts, offsets, object_re, object_im, probe_re, probe_im, frames, table)
-
-    strip = pltpu.VMEM((3 * rows, LANES), jnp.float32)
-    packed = f32(3 * rows // GROUPS, LANES)
+    )(*map(far, (object_re, object_im, probe_re, probe_im, frames, table)))
+
+    strip = pltpu.VMEM((layers * rows, LANES), jnp.float32)
+    packed = f32(2 * rows // GROUPS, LANES)
     cells, to_inner, to_outer = pl.pallas_call(
         row_halos,
         out_shape=(cells_shape, packed, packed),
-        in_specs=[VMEM] * 4,
+        in_specs=[VMEM] * 3,
         out_specs=(VMEM,) * 3,
         scratch_shapes=[strip],
         input_output_aliases={0: 0},
         compiler_params=PARAMS,
         name="row_halos",
-    )(cells, acc, by_inner, by_outer)
-    by_inner, by_outer = swap(to_inner, to_outer, "col")
+    )(cells, by_inner, by_outer)
+    by_inner, by_outer = swap(to_inner, to_outer, "col", False)
 
     order = pltpu.SMEM((slots,), jnp.int32)
     scalars = (counts, offsets, frame_index)
     acc = pl.pallas_call(
         windows_before,
         out_shape=acc_shape,
-        in_specs=[SMEM] * 3 + [VMEM] * 6,
+        in_specs=[SMEM] * 3 + [VMEM] * 5,
         out_specs=VMEM,
-        scratch_shapes=[order],
-        input_output_aliases={4: 0},
+        scratch_shapes=[order, pltpu.VMEM(probe_re.shape, jnp.float32)],
         compiler_params=PARAMS,
         cost_estimate=BUSY,
         name="windows_before",
-    )(*scalars, cells, acc, *fixed)
-
-    packed = f32(2 * rows // GROUPS, LANES)
+    )(*scalars, cells, *fixed)
+
+    packed = f32(layers * rows // GROUPS, LANES)
     cells, acc, to_inner, to_outer = pl.pallas_call(
         windows_over_edge,
         out_shape=(cells_shape, acc_shape, packed, packed),
@@ -523,7 +519,7 @@
         cost_estimate=BUSY,
         name="windows_over_edge",
     )(*scalars, cells, acc, *fixed, by_inner, by_outer)
-    by_inner, by_outer = swap(to_inner, to_outer, "col")
+    by_inner, by_outer = swap(to_inner, to_outer, "col", False)
 
     acc = pl.pallas_call(
         windows_after,
@@ -547,7 +543,7 @@
         compiler_params=PARAMS,
         name="row_spill",
     )(acc, by_inner, by_outer)
-    by_inner, by_outer = swap(to_inner, to_outer, "row")
+    by_inner, by_outer = swap(to_inner, to_outer, "row", True)
 
     return pl.pallas_call(
         finish,

time: 55.4 us -> 45.7 us (0.82)
  the two profiles are of different devices: /device:TPU:1 before, /device:TPU:9 now
where the time goes in v3:
time: 45.7 us; the launch traced here: 46.1 us
  Pallas kernels  20.3 us (44%)
  starting transfers between devices  12.1 us (26%)
  waiting for transfers between devices  5.11 us (11%)
  blocking collectives  4.2 us (9%)
  local copies, waits for them, and re-layouts  2.85 us (6%)
  between operations  1.46 us (3%)
    ppermute x4, starting transfers between devices, swap(): by_outer = lax.ppermute(to_outer, axis, outer + [(j, i) for i, j in outer])  11.8 us
    pallas_call x1, Pallas kernels, shards(): pl.pallas_call(windows_before, out_shape=acc_shape, in_specs=[SMEM] * 3 +...  6.99 us
    pallas_call x1, Pallas kernels, shards(): pl.pallas_call(windows_over_edge, out_shape=(cells_shape, acc_shape, pack...  5.31 us
    ppermute x4, waiting for transfers between devices, swap(): by_outer = lax.ppermute(to_outer, axis, outer + [(j, i) for i, j in outer])  4.59 us
    all_gather x2, blocking collectives, swap(): lax.all_gather(to_inner, axis, axis_index_groups=[list(pair) for pair in...  4.2 us
    unnamed x17, local copies, waits for them, and re-layouts  2.85 us
    pallas_call x1, Pallas kernels, shards(): pl.pallas_call(windows_after, out_shape=acc_shape, in_specs=[SMEM] * 3 +...  2.47 us
    pallas_call x1, Pallas kernels, shards(): pl.pallas_call(load_state, out_shape=(cells_shape, f32(*probe_re.shape),...  2.44 us
  transfers between devices with their start and end apart: 6, of which 3 were waited for; matrix products, arithmetic and copies ran while one was open for 0% of the time, Pallas kernels for 26%

profile of v3, /device:TPU:9, one launch (start us, length us, event | category | flops | bytes accessed | tf_op | source)
XLA Modules:
  0.0 46.1 jit_solution(5386402733483296321)
XLA Ops:
  0.6 1.0 %row_edges.1 = (f32[2,32,512]{2,1,0:T(8,128)S(1)}, f32[2,32,512]{2,1,0:T(8,128)S(1)}) custom-call(f32[384,512]{1,0:T(8,128)} %obj_re.3, f32[384,512]{1,0:T(8,128)} %obj_im.3), custom_call_target="tpu_custom_call" | custom-call | tf_op jit(solution)/shard_map/row_edges/pallas_call | solution.py:458
  1.6 3.7 %collective-permute-start = (f32[2,32,512]{2,1,0:T(8,128)S(1)}, f32[2,32,512]{2,1,0:T(8,128)S(1)}, u32[]{:S(2)}, u32[]{:S(2)}) collective-permute-start(f32[2,32,512]{2,1,0:T(8,128)S(1)} %get-tuple-element.21), channel_id=1, source_target_pairs={{4,8},{12,16},{20,24},{8,4},{16,12},{24,20},{5,9},{13,17},{21,25},... | collective-permute-start | bytes 393224 | tf_op jit(solution)/shard_map/ppermute | solution.py:431
  5.3 0.0 copy-start.7
  5.3 2.4 %load_state.1 = (f32[2,448,768]{2,1,0:T(8,128)S(1)}, f32[256,256]{1,0:T(8,128)S(1)}, f32[256,256]{1,0:T(8,128)S(1)}, bf16[8,256,256]{2,1,0:T(8,128)(2,1)S(1)}, bf16[10,256,256]{2,1,0:T(8,128)(2,1)S(1)}) custom-call(f32[384,512]{1,0:T(8,128)} %obj_re.3, f32[384,512]{1,0:T(8,128)} %obj_im.3, f32[256,256]{1,0:T(8,128)} %probe_re_far.1, ...), custom_call_target="tpu_custom_call" | custom-call | flops 4000000000 | bytes 8000000 | tf_op jit(solution)/shard_map/load_state/pallas_call | solution.py:469
  7.8 0.0 copy-start.1
  7.8 1.1 %copy-done.1 = bf16[10,256,256]{2,1,0:T(8,128)(2,1)} copy-done((bf16[10,256,256]{2,1,0:T(8,128)(2,1)}, bf16[10,256,256]{2,1,0:T(8,128)(2,1)S(1)}, u32[]{:S(2)}) %copy-start.1) | copy-done | bytes 1310744
  8.9 0.0 copy-start.3
  8.9 1.0 %copy-done.3 = bf16[8,256,256]{2,1,0:T(8,128)(2,1)} copy-done((bf16[8,256,256]{2,1,0:T(8,128)(2,1)}, bf16[8,256,256]{2,1,0:T(8,128)(2,1)S(1)}, u32[]{:S(2)}) %copy-start.3) | copy-done | bytes 1048600
  9.8 0.0 copy-start.5
  9.8 0.7 %copy-done.5 = f32[256,256]{1,0:T(8,128)} copy-done((f32[256,256]{1,0:T(8,128)}, f32[256,256]{1,0:T(8,128)S(1)}, u32[]{:S(2)}) %copy-start.5) | copy-done | bytes 262168
  10.5 0.0 copy-start
  11.2 0.0 copy-done.7
  11.2 0.1 copy.20.offsets
  11.3 0.0 copy-start.2
  11.3 0.0 copy-start.4
  11.3 0.0 copy-start.6
  11.3 2.1 %all-gather = f32[4,32,512]{2,1,0:T(8,128)S(1)} all-gather(f32[2,32,512]{2,1,0:T(8,128)S(1)} %get-tuple-element.20), channel_id=2, replica_groups={{0,4},{8,12},{16,20},{24,28},{1,5},{9,13},{17,21},{25,29},{2,6},{10,14}..., dimensions={0}, use_global_device_ids=true | all-gather | bytes 393216 | tf_op jit(solution)/shard_map/all_gather | solution.py:433
  13.4 0.0 collective-permute-done.by_outer
  13.4 0.2 row_halos.1
  13.7 0.2 collective-permute-start.1
  13.9 4.3 %collective-permute-start.2 = (f32[224,128]{1,0:T(8,128)S(1)}, f32[224,128]{1,0:T(8,128)S(1)}, u32[]{:S(2)}, u32[]{:S(2)}) collective-permute-start(f32[224,128]{1,0:T(8,128)S(1)} %get-tuple-element.28), channel_id=1, source_target_pairs={{1,2},{2,1},{5,6},{6,5},{9,10},{10,9},{13,14},{14,13},{17,18},{18,... | collective-permute-start | bytes 344072 | tf_op jit(solution)/shard_map/ppermute | solution.py:431
  18.2 0.0 copy-done
  18.2 0.0 copy-done.2
  18.2 0.0 copy-done.4
  18.3 0.0 copy-done.6
  18.3 7.0 %windows_before.1.acc_in = f32[3,448,768]{2,1,0:T(8,128)S(1)} custom-call(s32[1,1]{1,0:T(1,128)S(6)} %copy.27.counts, s32[1,1,8,2]{3,2,1,0:T(8,128)S(1)} %copy.20.offsets, s32[1,1,8]{2,1,0:T(1,128)S(1)} %copy-done, f32[2,448,768]{2,1,0:T(8,128)S(1)} %get-tuple-element.22.cells.cells_in, f32[256,256]{1,0:T(8,128)S(1)} %get-tuple-element.23.probe_re, ...), custom_call_target="tpu_custom_call" | custom-call | flops 4000000000 | bytes 8000000 | tf_op jit(solution)/shard_map/windows_before/pallas_call | solution.py:499
  25.3 0.0 collective-permute-done.1.by_inner
  25.3 0.0 collective-permute-done.2.by_outer
  25.3 5.3 %windows_over_edge.1 = (f32[2,448,768]{2,1,0:T(8,128)S(1)}, f32[3,448,768]{2,1,0:T(8,128)S(1)}, f32[336,128]{1,0:T(8,128)S(1)}, f32[336,128]{1,0:T(8,128)S(1)}) custom-call(s32[1,1]{1,0:T(1,128)S(6)} %copy.27.counts, s32[1,1,8,2]{3,2,1,0:T(8,128)S(1)} %copy.20.offsets, s32[1,1,8]{2,1,0:T(1,128)S(1)} %copy-done, ...), custom_call_target="tpu_custom_call", output_to_operand_aliasing={{0}: (3, {}), {1}: (4, {})} | custom-call | flops 4000000000 | bytes 8000000 | tf_op jit(solution)/shard_map/windows_over_edge/pallas_call | solution.py:511
  30.6 0.1 collective-permute-start.3
  30.7 1.9 %collective-permute-start.4 = (f32[336,128]{1,0:T(8,128)S(1)}, f32[336,128]{1,0:T(8,128)S(1)}, u32[]{:S(2)}, u32[]{:S(2)}) collective-permute-start(f32[336,128]{1,0:T(8,128)S(1)} %get-tuple-element.32), channel_id=1, source_target_pairs={{1,2},{2,1},{5,6},{6,5},{9,10},{10,9},{13,14},{14,13},{17,18},{18,... | collective-permute-start | bytes 516104 | tf_op jit(solution)/shard_map/ppermute | solution.py:431
  32.6 2.5 %windows_after.1.acc_in = f32[3,448,768]{2,1,0:T(8,128)S(1)} custom-call(s32[1,1]{1,0:T(1,128)S(6)} %copy.27.counts, s32[1,1,8,2]{3,2,1,0:T(8,128)S(1)} %copy.20.offsets, s32[1,1,8]{2,1,0:T(1,128)S(1)} %copy-done, f32[2,448,768]{2,1,0:T(8,128)S(1)} %get-tuple-element.29.cells, ...), custom_call_target="tpu_custom_call", output_to_operand_aliasing={{}: (4, {})} | custom-call | flops 4000000000 | bytes 8000000 | tf_op jit(solution)/shard_map/windows_after/pallas_call | solution.py:524
  35.1 0.5 %collective-permute-done.3.by_inner = f32[336,128]{1,0:T(8,128)S(1)} collective-permute-done((f32[336,128]{1,0:T(8,128)S(1)}, f32[336,128]{1,0:T(8,128)S(1)}, u32[]{:S(2)}, u32[]{:S(2)}) %collective-permute-start.3) | collective-permute-done | bytes 172064 | tf_op jit(solution)/shard_map/ppermute | solution.py:435
  35.6 1.6 %collective-permute-done.4.by_outer = f32[336,128]{1,0:T(8,128)S(1)} collective-permute-done((f32[336,128]{1,0:T(8,128)S(1)}, f32[336,128]{1,0:T(8,128)S(1)}, u32[]{:S(2)}, u32[]{:S(2)}) %collective-permute-start.4) | collective-permute-done | bytes 172064 | tf_op jit(solution)/shard_map/ppermute | solution.py:431
  37.2 0.4 row_spill.1
  37.6 1.9 %collective-permute-start.5 = (f32[3,32,512]{2,1,0:T(8,128)S(1)}, f32[3,32,512]{2,1,0:T(8,128)S(1)}, u32[]{:S(2)}, u32[]{:S(2)}) collective-permute-start(f32[3,32,512]{2,1,0:T(8,128)S(1)} %get-tuple-element.35), channel_id=1, source_target_pairs={{4,8},{12,16},{20,24},{8,4},{16,12},{24,20},{5,9},{13,17},{21,25},... | collective-permute-start | bytes 589832 | tf_op jit(solution)/shard_map/ppermute | solution.py:431
  39.5 2.1 %all-gather.1 = f32[6,32,512]{2,1,0:T(8,128)S(1)} all-gather(f32[3,32,512]{2,1,0:T(8,128)S(1)} %get-tuple-element.34), channel_id=3, replica_groups={{0,4},{8,12},{16,20},{24,28},{1,5},{9,13},{17,21},{25,29},{2,6},{10,14}..., dimensions={0}, use_global_device_ids=true | all-gather | bytes 589824 | tf_op jit(solution)/shard_map/all_gather | solution.py:433
  41.6 3.0 %collective-permute-done.5.by_outer = f32[3,32,512]{2,1,0:T(8,128)S(1)} collective-permute-done((f32[3,32,512]{2,1,0:T(8,128)S(1)}, f32[3,32,512]{2,1,0:T(8,128)S(1)}, u32[]{:S(2)}, u32[]{:S(2)}) %collective-permute-start.5) | collective-permute-done | bytes 196640 | tf_op jit(solution)/shard_map/ppermute | solution.py:431
  44.6 1.5 %finish.1 = (f32[384,512]{1,0:T(8,128)}, f32[384,512]{1,0:T(8,128)}) custom-call(f32[2,448,768]{2,1,0:T(8,128)S(1)} %get-tuple-element.29.cells, f32[3,448,768]{2,1,0:T(8,128)S(1)} %get-tuple-element.33.acc, f32[2,3,32,512]{3,2,1,0:T(8,128)S(1)} %bitcast.3, f32[3,32,512]{2,1,0:T(8,128)S(1)} %collective-permute-done.5.by_outer), custom_call_target="tpu_custom_call" | custom-call | tf_op jit(solution)/shard_map/finish/pallas_call | solution.py:548
Async XLA Ops:
  1.6 11.8 %collective-permute-start = (f32[2,32,512]{2,1,0:T(8,128)S(1)}, f32[2,32,512]{2,1,0:T(8,128)S(1)}, u32[]{:S(2)}, u32[]{:S(2)}) collective-permute-start(f32[2,32,512]{2,1,0:T(8,128)S(1)} %get-tuple-element.21), channel_id=1, source_target_pairs={{4,8},{12,16},{20,24},{8,4},{16,12},{24,20},{5,9},{13,17},{21,25},... | collective-permute-start | bytes 393224 | tf_op jit(solution)/shard_map/ppermute | solution.py:431
  5.3 5.9 %copy-start.7 = (s32[1,1,8,2]{2,3,1,0:T(2,128)S(1)}, s32[1,1,8,2]{2,3,1,0:T(2,128)}, u32[]{:S(2)}) copy-start(s32[1,1,8,2]{2,3,1,0:T(2,128)} %param.15) | copy-start | bytes 196
  7.8 1.1 %copy-start.1 = (bf16[10,256,256]{2,1,0:T(8,128)(2,1)}, bf16[10,256,256]{2,1,0:T(8,128)(2,1)S(1)}, u32[]{:S(2)}) copy-start(bf16[10,256,256]{2,1,0:T(8,128)(2,1)S(1)} %get-tuple-element.26.table) | copy-start | bytes 3932164
  8.9 1.0 %copy-start.3 = (bf16[8,256,256]{2,1,0:T(8,128)(2,1)}, bf16[8,256,256]{2,1,0:T(8,128)(2,1)S(1)}, u32[]{:S(2)}) copy-start(bf16[8,256,256]{2,1,0:T(8,128)(2,1)S(1)} %get-tuple-element.25.frames) | copy-start | bytes 3145732
  9.8 0.7 %copy-start.5 = (f32[256,256]{1,0:T(8,128)}, f32[256,256]{1,0:T(8,128)S(1)}, u32[]{:S(2)}) copy-start(f32[256,256]{1,0:T(8,128)S(1)} %get-tuple-element.24.probe_im) | copy-start | bytes 786436
  10.5 7.7 %copy-start = (s32[1,1,8]{2,1,0:T(1,128)S(1)}, s32[1,1,8]{2,1,0:T(1,128)}, u32[]{:S(2)}) copy-start(s32[1,1,8]{2,1,0:T(1,128)} %chosen.5) | copy-start | bytes 100
  11.3 7.0 %copy-start.2 = (bf16[10,256,256]{2,1,0:T(8,128)(2,1)S(1)}, bf16[10,256,256]{2,1,0:T(8,128)(2,1)}, u32[]{:S(2)}) copy-start(bf16[10,256,256]{2,1,0:T(8,128)(2,1)} %copy-done.1) | copy-start | bytes 3932164
  11.3 7.0 %copy-start.4 = (bf16[8,256,256]{2,1,0:T(8,128)(2,1)S(1)}, bf16[8,256,256]{2,1,0:T(8,128)(2,1)}, u32[]{:S(2)}) copy-start(bf16[8,256,256]{2,1,0:T(8,128)(2,1)} %copy-done.3) | copy-start | bytes 3145732
  11.3 7.0 %copy-start.6 = (f32[256,256]{1,0:T(8,128)S(1)}, f32[256,256]{1,0:T(8,128)}, u32[]{:S(2)}) copy-start(f32[256,256]{1,0:T(8,128)} %copy-done.5) | copy-start | bytes 786436
  13.7 11.6 %collective-permute-start.1 = (f32[224,128]{1,0:T(8,128)S(1)}, f32[224,128]{1,0:T(8,128)S(1)}, u32[]{:S(2)}, u32[]{:S(2)}) collective-permute-start(f32[224,128]{1,0:T(8,128)S(1)} %get-tuple-element.27), channel_id=1, source_target_pairs={{0,1},{2,3},{1,0},{3,2},{4,5},{6,7},{5,4},{7,6},{8,9},{10,11},{9,8... | collective-permute-start | bytes 344072 | tf_op jit(solution)/shard_map/ppermute | solution.py:435
  13.9 11.4 %collective-permute-start.2 = (f32[224,128]{1,0:T(8,128)S(1)}, f32[224,128]{1,0:T(8,128)S(1)}, u32[]{:S(2)}, u32[]{:S(2)}) collective-permute-start(f32[224,128]{1,0:T(8,128)S(1)} %get-tuple-element.28), channel_id=1, source_target_pairs={{1,2},{2,1},{5,6},{6,5},{9,10},{10,9},{13,14},{14,13},{17,18},{18,... | collective-permute-start | bytes 344072 | tf_op jit(solution)/shard_map/ppermute | solution.py:431
  30.6 5.0 %collective-permute-start.3 = (f32[336,128]{1,0:T(8,128)S(1)}, f32[336,128]{1,0:T(8,128)S(1)}, u32[]{:S(2)}, u32[]{:S(2)}) collective-permute-start(f32[336,128]{1,0:T(8,128)S(1)} %get-tuple-element.31), channel_id=1, source_target_pairs={{0,1},{2,3},{1,0},{3,2},{4,5},{6,7},{5,4},{7,6},{8,9},{10,11},{9,8... | collective-permute-start | bytes 516104 | tf_op jit(solution)/shard_map/ppermute | solution.py:435
  30.7 6.5 %collective-permute-start.4 = (f32[336,128]{1,0:T(8,128)S(1)}, f32[336,128]{1,0:T(8,128)S(1)}, u32[]{:S(2)}, u32[]{:S(2)}) collective-permute-start(f32[336,128]{1,0:T(8,128)S(1)} %get-tuple-element.32), channel_id=1, source_target_pairs={{1,2},{2,1},{5,6},{6,5},{9,10},{10,9},{13,14},{14,13},{17,18},{18,... | collective-permute-start | bytes 516104 | tf_op jit(solution)/shard_map/ppermute | solution.py:431
  37.6 7.0 %collective-permute-start.5 = (f32[3,32,512]{2,1,0:T(8,128)S(1)}, f32[3,32,512]{2,1,0:T(8,128)S(1)}, u32[]{:S(2)}, u32[]{:S(2)}) collective-permute-start(f32[3,32,512]{2,1,0:T(8,128)S(1)} %get-tuple-element.35), channel_id=1, source_target_pairs={{4,8},{12,16},{20,24},{8,4},{16,12},{24,20},{5,9},{13,17},{21,25},... | collective-permute-start | bytes 589832 | tf_op jit(solution)/shard_map/ppermute | solution.py:431
